TPU v7x, 256 devices: a whole 4x4x8 slice. The times are simulated.
256 devices in a mesh: ctx: 32 (over z_lo, x, core), tp: 8 (over y, z_hi).
Axes of the slice: x: 4, y: 4, z: 8 (z_hi: 2, z_lo: 4; z = z_hi * 4 + z_lo), core: 2. Of those that a mesh axis runs over, the one named last changes fastest.
Arguments:
- query_feat: bfloat16 [8192, 24576], P('tp', 'ctx'), may hold values from -6 to 6
- key_feat: bfloat16 [8192, 24576], P('tp', 'ctx'), may hold values from -6 to 6
- value_feat: bfloat16 [8192, 24576], P('tp', 'ctx'), may hold values from -6 to 6
- grad_out: bfloat16 [8192, 24576], P('tp', 'ctx'), may hold values from -6 to 6
- short_taps: float32 [3, 3, 8192], P(None, None, 'tp'), may hold values from -3 to 3
- filters: bfloat16 [512, 128], P(('tp', 'ctx')), may hold values from -0.48 to 0.48
- skip_bias: bfloat16 [8192], P(('tp', 'ctx')), may hold values from 0.5 to 1.5
Outputs:
- grad_query: bfloat16 [8192, 24576], P('tp', 'ctx')
- grad_key: bfloat16 [8192, 24576], P('tp', 'ctx')
- grad_value: bfloat16 [8192, 24576], P('tp', 'ctx')
- grad_short: float32 [3, 3, 8192], P(None, None, 'tp')
- grad_filters: float32 [512, 128], P(('tp', 'ctx'))
- grad_bias: float32 [8192], P(('tp', 'ctx'))
All inputs are finite; a program needn't handle non-finite values.
Results may differ from a plain program's by a relative error of at most 0.019.
Values may be sent and summed in bfloat16 or wider, within the bound.
A program may use at most 192 MiB of HBM per device.

v0:
```python
import jax
import jax.numpy as jnp
import numpy as np
from jax import lax
from jax.sharding import PartitionSpec as P

TAPS = 128
SHORT = 3


def shifted(block, axis, distance):
    devices = range(lax.axis_size(axis))
    route = [(i - distance, i) for i in devices if i - distance in devices]
    return lax.ppermute(block, axis, route)


def toeplitz(filt):
    rows = np.arange(2 * TAPS)[:, None]
    cols = np.arange(TAPS)[None, :]
    offset = cols - rows + TAPS
    valid = (offset >= 0) & (offset < TAPS)
    picked = jnp.take(filt, np.clip(offset, 0, TAPS - 1).reshape(-1), axis=1)
    picked = picked.reshape(filt.shape[0], 2 * TAPS, TAPS)
    return jnp.where(valid[None], picked, jnp.zeros((), filt.dtype))


def diagonal_sums(difference_matrix):
    groups = difference_matrix.shape[0]
    flipped = difference_matrix[:, ::-1, :]
    padded = jnp.pad(flipped, ((0, 0), (0, 0), (0, 2 * TAPS)))
    skewed = padded.reshape(groups, -1)[:, : 2 * TAPS * (3 * TAPS - 1)]
    skewed = skewed.reshape(groups, 2 * TAPS, 3 * TAPS - 1)
    totals = jnp.sum(skewed, axis=1)
    return totals[:, TAPS - 1 : 2 * TAPS - 1]


def short_forward(signal, rim, taps):
    length = signal.shape[1]
    lengthened_input = jnp.concatenate([rim, signal], 1)
    total = jnp.zeros(signal.shape, jnp.float32)
    for offset in range(SHORT):
        start = SHORT - 1 - offset
        total = total + taps[offset][:, None] * lengthened_input[:, start : start + length].astype(
            jnp.float32
        )
    return (total.astype(jnp.bfloat16), lengthened_input)


def short_backward(grad, rim_next, taps, lengthened_input):
    length = grad.shape[1]
    ext_grad = jnp.concatenate([grad, rim_next], 1)
    total = jnp.zeros(grad.shape, jnp.float32)
    tap_terms = []
    for offset in range(SHORT):
        total = total + taps[offset][:, None] * ext_grad[:, offset : offset + length].astype(
            jnp.float32
        )
        start = SHORT - 1 - offset
        tap_terms.append(
            jnp.sum(
                grad.astype(jnp.float32)
                * lengthened_input[:, start : start + length].astype(jnp.float32),
                axis=1,
            )
        )
    return (total.astype(jnp.bfloat16), jnp.stack(tap_terms))


def mix_forward(query_conv, product, grad_out, filter_matrix, bias, before):
    channels, length = product.shape
    groups = filter_matrix.shape[0]
    blocks = length // TAPS
    reshaped_rows = product.reshape(groups, channels // groups, blocks, TAPS)
    prior = jnp.concatenate(
        [before.reshape(groups, channels // groups, 1, TAPS), reshaped_rows[:, :, :-1]], 2
    )
    stacked_rows = jnp.concatenate([prior, reshaped_rows], 3)
    causal_filtering = jnp.einsum(
        "qpxy,qyf->qpxf", stacked_rows, filter_matrix, preferred_element_type=jnp.float32
    )
    bias_col = bias.astype(jnp.float32)[:, None]
    mixed = causal_filtering.reshape(channels, length) + bias_col * product.astype(jnp.float32)
    grad_mixed = (grad_out.astype(jnp.float32) * query_conv.astype(jnp.float32)).astype(
        jnp.bfloat16
    )
    grad_qconv = (grad_out.astype(jnp.float32) * mixed).astype(jnp.bfloat16)
    return (stacked_rows, grad_mixed, grad_qconv)


def mix_backward(stacked_rows, product, grad_mixed, filter_matrix, bias, after):
    channels, length = product.shape
    groups = filter_matrix.shape[0]
    blocks = length // TAPS
    reshaped_rows = grad_mixed.reshape(groups, channels // groups, blocks, TAPS)
    lengthened_input = jnp.concatenate(
        [reshaped_rows, after.reshape(groups, channels // groups, 1, TAPS)], 2
    )
    reverse_pass = jnp.einsum(
        "hxvp,hop->hxvo", lengthened_input, filter_matrix, preferred_element_type=jnp.float32
    )
    bias_col = bias.astype(jnp.float32)[:, None]
    conv_grad = (reverse_pass[:, :, :-1, TAPS:] + reverse_pass[:, :, 1:, :TAPS]).reshape(
        channels, length
    )
    grad_product = (conv_grad + bias_col * grad_mixed.astype(jnp.float32)).astype(jnp.bfloat16)
    difference_matrix = jnp.einsum(
        "finp,finl->fpl", stacked_rows, reshaped_rows, preferred_element_type=jnp.float32
    )
    bias_grad = jnp.sum(grad_mixed.astype(jnp.float32) * product.astype(jnp.float32), axis=1)
    return (grad_product, diagonal_sums(difference_matrix), bias_grad)


def times_bf(first, second):
    return (first.astype(jnp.float32) * second.astype(jnp.float32)).astype(jnp.bfloat16)


def body(query_feat, key_feat, value_feat, grad_out, short_taps, filters, skip_bias):
    channels, length = query_feat.shape
    edge = length - (SHORT - 1)
    rims = shifted((query_feat[:, edge:], key_feat[:, edge:], value_feat[:, edge:]), "ctx", 1)
    query_conv, query_ext = short_forward(query_feat, rims[0], short_taps[0])
    key_conv, key_ext = short_forward(key_feat, rims[1], short_taps[1])
    value_conv, value_ext = short_forward(value_feat, rims[2], short_taps[2])
    filter_matrix = toeplitz(filters)
    query_grp, key_grp, value_grp, cotan_grp = (
        lax.all_to_all(query_conv, "ctx", split_axis=0, concat_axis=1, tiled=True),
        lax.all_to_all(key_conv, "ctx", split_axis=0, concat_axis=1, tiled=True),
        lax.all_to_all(value_conv, "ctx", split_axis=0, concat_axis=1, tiled=True),
        lax.all_to_all(grad_out, "ctx", split_axis=0, concat_axis=1, tiled=True),
    )
    blank = jnp.zeros((query_grp.shape[0], TAPS), jnp.bfloat16)
    product_grp = times_bf(key_grp, value_grp)
    stacked_rows, grad_mixed, grad_qgrp = mix_forward(
        query_grp, product_grp, cotan_grp, filter_matrix, skip_bias, blank
    )
    grad_pgrp, grad_filters, grad_bias = mix_backward(
        stacked_rows, product_grp, grad_mixed, filter_matrix, skip_bias, blank
    )
    grad_kgrp = times_bf(grad_pgrp, value_grp)
    grad_vgrp = times_bf(grad_pgrp, key_grp)
    grad_qconv, grad_kconv, grad_vconv = (
        lax.all_to_all(grad_qgrp, "ctx", split_axis=1, concat_axis=0, tiled=True),
        lax.all_to_all(grad_kgrp, "ctx", split_axis=1, concat_axis=0, tiled=True),
        lax.all_to_all(grad_vgrp, "ctx", split_axis=1, concat_axis=0, tiled=True),
    )
    next_rims = shifted(
        (grad_qconv[:, : SHORT - 1], grad_kconv[:, : SHORT - 1], grad_vconv[:, : SHORT - 1]),
        "ctx",
        -1,
    )
    grad_query, tap_query = short_backward(grad_qconv, next_rims[0], short_taps[0], query_ext)
    grad_key, tap_key = short_backward(grad_kconv, next_rims[1], short_taps[1], key_ext)
    grad_value, tap_value = short_backward(grad_vconv, next_rims[2], short_taps[2], value_ext)
    grad_short = lax.psum(jnp.stack([tap_query, tap_key, tap_value]), "ctx")
    return (grad_query, grad_key, grad_value, grad_short, grad_filters, grad_bias)


def solution(mesh):
    in_specs = (
        P("tp", "ctx"),
        P("tp", "ctx"),
        P("tp", "ctx"),
        P("tp", "ctx"),
        P(None, None, "tp"),
        P(("tp", "ctx"), None),
        P(("tp", "ctx")),
    )
    out_specs = (
        P("tp", "ctx"),
        P("tp", "ctx"),
        P("tp", "ctx"),
        P(None, None, "tp"),
        P(("tp", "ctx"), None),
        P(("tp", "ctx")),
    )
    return jax.shard_map(body, mesh=mesh, in_specs=in_specs, out_specs=out_specs, check_vma=False)
```

profile of v0, /device:TPU:1, one launch (start us, length us, event | category | flops | bytes accessed | tf_op | source)
XLA Modules:
  0.0 621.2 jit_solution(9098958094956435440)
XLA Ops:
  0.7 10.2 %all-to-all-start = ((bf16[32,32,768]{2,1,0:T(8,128)(2,1)}), bf16[32,32,768]{2,1,0:T(8,128)(2,1)S(1)}, u32[]{:S(2)}, u32[]{:S(2)}) async-start(bf16[32,32,768]{2,1,0:T(8,128)(2,1)} %bitcast.139), calls=%async_computation | async-start | bytes 3145728 | tf_op jit(solution)/shard_map/all_to_all | solution.py:129
  10.8 0.1 slice.154
  11.0 3.5 collective-permute-start.3
  14.6 9.8 %collective-permute-done.3 = bf16[1024,2]{1,0:T(8,128)(2,1)S(1)} collective-permute-done((bf16[1024,2]{1,0:T(8,128)(2,1)S(1)}, bf16[1024,2]{1,0:T(8,128)(2,1)S(1)}, u32[]{:S(2)}, u32[]{:S(2)}) %collective-permute-start.3) | collective-permute-done | bytes 4128 | tf_op jit(solution)/shard_map/ppermute | solution.py:14
  24.3 0.7 copy-done.7
  25.0 3.0 fusion.15
  28.0 19.7 %all-to-all-done = bf16[32,32,768]{2,1,0:T(8,128)(2,1)S(1)} async-done(((bf16[32,32,768]{2,1,0:T(8,128)(2,1)}), bf16[32,32,768]{2,1,0:T(8,128)(2,1)S(1)}, u32[]{:S(2)}, u32[]{:S(2)}) %all-to-all-start) | async-done | bytes 1572896 | tf_op jit(solution)/shard_map/all_to_all | solution.py:129
  47.7 11.5 %all-to-all-start.4 = ((bf16[32,32,768]{2,1,0:T(8,128)(2,1)}), bf16[32,32,768]{2,1,0:T(8,128)(2,1)S(1)}, u32[]{:S(2)}, u32[]{:S(2)}) async-start(bf16[32,32,768]{2,1,0:T(8,128)(2,1)} %bitcast.137), calls=%async_computation.4 | async-start | bytes 3145728 | tf_op jit(solution)/shard_map/all_to_all | solution.py:126
  59.2 1.1 slice.138
  60.3 3.5 collective-permute-start
  63.9 8.9 %collective-permute-done = bf16[1024,2]{1,0:T(8,128)(2,1)S(1)} collective-permute-done((bf16[1024,2]{1,0:T(8,128)(2,1)S(1)}, bf16[1024,2]{1,0:T(8,128)(2,1)S(1)}, u32[]{:S(2)}, u32[]{:S(2)}) %collective-permute-start) | collective-permute-done | bytes 4128 | tf_op jit(solution)/shard_map/ppermute | solution.py:14
  72.7 0.7 copy-done.9
  73.4 6.1 fusion.6
  79.6 16.5 %all-to-all-done.4 = bf16[32,32,768]{2,1,0:T(8,128)(2,1)S(1)} async-done(((bf16[32,32,768]{2,1,0:T(8,128)(2,1)}), bf16[32,32,768]{2,1,0:T(8,128)(2,1)S(1)}, u32[]{:S(2)}, u32[]{:S(2)}) %all-to-all-start.4) | async-done | bytes 1572896 | tf_op jit(solution)/shard_map/all_to_all | solution.py:126
  96.1 14.7 %all-to-all-start.1 = ((bf16[32,32,768]{2,1,0:T(8,128)(2,1)}), bf16[32,32,768]{2,1,0:T(8,128)(2,1)S(1)}, u32[]{:S(2)}, u32[]{:S(2)}) async-start(bf16[32,32,768]{2,1,0:T(8,128)(2,1)} %bitcast.136), calls=%async_computation.1 | async-start | bytes 3145728 | tf_op jit(solution)/shard_map/all_to_all | solution.py:127
  110.8 1.1 slice.144
  111.9 3.5 collective-permute-start.1
  115.4 8.9 %collective-permute-done.1 = bf16[1024,2]{1,0:T(8,128)(2,1)S(1)} collective-permute-done((bf16[1024,2]{1,0:T(8,128)(2,1)S(1)}, bf16[1024,2]{1,0:T(8,128)(2,1)S(1)}, u32[]{:S(2)}, u32[]{:S(2)}) %collective-permute-start.1) | collective-permute-done | bytes 4128 | tf_op jit(solution)/shard_map/ppermute | solution.py:14
  124.3 0.7 copy-done.10
  125.0 6.3 %fusion.9 = bf16[1024,768]{1,0:T(8,128)(2,1)} fusion(bf16[1024,768]{1,0:T(8,128)(2,1)} %param.11, bf16[1024,2]{1,0:T(8,128)(2,1)S(1)} %collective-permute-done.1, f32[1024]{0:T(1024)S(1)} %bitcast.150, f32[1024]{0:T(1024)S(1)} %bitcast.152, f32[1024]{0:T(1024)S(1)} %bitcast.154), kind=kLoop, calls=%fused_computation.43 | loop fusion | flops 11796480 | bytes 3162112 | tf_op jit(solution)/shard_map/convert_element_type | solution.py:46
  131.4 16.3 %all-to-all-done.1 = bf16[32,32,768]{2,1,0:T(8,128)(2,1)S(1)} async-done(((bf16[32,32,768]{2,1,0:T(8,128)(2,1)}), bf16[32,32,768]{2,1,0:T(8,128)(2,1)S(1)}, u32[]{:S(2)}, u32[]{:S(2)}) %all-to-all-start.1) | async-done | bytes 1572896 | tf_op jit(solution)/shard_map/all_to_all | solution.py:127
  147.7 14.9 %all-to-all-start.2 = ((bf16[32,32,768]{2,1,0:T(8,128)(2,1)}), bf16[32,32,768]{2,1,0:T(8,128)(2,1)S(1)}, u32[]{:S(2)}, u32[]{:S(2)}) async-start(bf16[32,32,768]{2,1,0:T(8,128)(2,1)} %bitcast.135), calls=%async_computation.2 | async-start | bytes 3145728 | tf_op jit(solution)/shard_map/all_to_all | solution.py:128
  162.6 0.1 copy.34
  162.8 115.0 %gather_fusion = bf16[32768,2]{1,0:T(8,128)(2,1)} fusion(bf16[2,128]{0,1:T(8,128)(2,1)S(1)} %copy.34, s32[32768]{0:T(1024)S(1)} %broadcast_clamp_fusion), kind=kCustom, calls=%fused_computation | custom fusion | bytes 393216 | tf_op jit(solution)/shard_map/jit(_take)/gather | solution.py:22
  277.8 7.0 %copy.35 = bf16[2,256,128]{2,1,0:T(8,128)(2,1)S(1)} copy(bf16[2,256,128]{0,2,1:T(8,128)(2,1)} %bitcast.134) | data formatting | bytes 262144 | tf_op jit(solution)/shard_map/jit(_take)/gather | solution.py:22
  284.8 2.0 fusion.51
  286.8 2.0 copy.37
  288.8 4.0 convert_element_type.256
  292.8 2.0 fusion.52
  294.8 0.0 copy-start.11
  294.8 2.0 copy.33
  296.8 4.0 convert_element_type.235
  300.8 4.6 fusion.55
  305.4 4.6 reshape.115
  310.0 2.5 fusion.43
  312.5 2.2 slice_add_fusion
  314.6 4.7 reshape.116
  319.3 10.1 %fusion.18 = (f32[32]{0:T(128)}, bf16[32,32,768]{2,0,1:T(8,128)(2,1)S(1)}, bf16[32,32,768]{2,0,1:T(8,128)(2,1)}, bf16[32,32,768]{2,0,1:T(8,128)(2,1)}) fusion(bf16[32,32,768]{2,1,0:T(8,128)(2,1)} %copy-done.3, bf16[32,32,768]{2,1,0:T(8,128)(2,1)S(1)} %copy-done.2, bf16[32,32,768]{2,1,0:T(8,128)(2,1)S(1)} %all-to-all-done.2, ...), kind=kLoop, calls=%fused_computation.52 | loop fusion | flops 17301472 | bytes 17301760 | tf_op jit(solution)/shard_map/reduce_sum | solution.py:109
  329.3 46.5 %all_to_all.100 = bf16[32,32,768]{2,0,1:T(8,128)(2,1)} all-to-all(bf16[32,32,768]{2,0,1:T(8,128)(2,1)S(1)} %get-tuple-element.18), channel_id=1, replica_groups=mesh['ctx'=32,'tp'=8] {'ctx'}, dimensions={1} | all-to-all | bytes 3145728 | tf_op jit(solution)/shard_map/all_to_all | solution.py:142
  375.8 4.2 all-to-all-start.6
  380.0 3.1 fusion.19
  383.1 33.8 %all-to-all-done.6 = bf16[32,32,768]{2,0,1:T(8,128)(2,1)S(1)} async-done(((bf16[32,32,768]{2,0,1:T(8,128)(2,1)}), bf16[32,32,768]{2,0,1:T(8,128)(2,1)S(1)}, u32[]{:S(2)}, u32[]{:S(2)}) %all-to-all-start.6) | async-done | bytes 1572896 | tf_op jit(solution)/shard_map/all_to_all | solution.py:144
  416.9 6.2 %all-to-all-start.5 = ((bf16[32,32,768]{2,0,1:T(8,128)(2,1)}), bf16[32,32,768]{2,0,1:T(8,128)(2,1)S(1)}, u32[]{:S(2)}, u32[]{:S(2)}) async-start(bf16[32,32,768]{2,0,1:T(8,128)(2,1)} %fusion.19), calls=%async_computation.5 | async-start | bytes 3145728 | tf_op jit(solution)/shard_map/all_to_all | solution.py:143
  423.1 4.4 fusion.57
  427.6 1.7 rev.3
  429.3 0.1 pad_bitcast_fusion
  429.4 0.6 copy.41
  430.0 0.9 slice.187
  430.9 3.2 reshape.118
  434.1 1.2 reduce_sum.108
  435.3 0.0 copy-start.6
  435.3 0.6 slice.188
  435.9 2.0 slice.174
  437.9 2.1 collective-permute-start.2
  440.0 5.8 fusion.40
  445.9 2.4 fusion.28
  448.3 11.8 %all-to-all-done.5 = bf16[32,32,768]{2,0,1:T(8,128)(2,1)S(1)} async-done(((bf16[32,32,768]{2,0,1:T(8,128)(2,1)}), bf16[32,32,768]{2,0,1:T(8,128)(2,1)S(1)}, u32[]{:S(2)}, u32[]{:S(2)}) %all-to-all-start.5) | async-done | bytes 1572896 | tf_op jit(solution)/shard_map/all_to_all | solution.py:143
  460.0 5.6 fusion.34
  465.7 131.1 %psum.7 = f32[3,3,1024]{2,1,0:T(4,128)} all-reduce(f32[3,3,1024]{2,1,0:T(4,128)S(1)} %pad_maximum_fusion.6), channel_id=1, replica_groups=mesh['ctx'=32,'tp'=8] {'ctx'}, use_global_device_ids=true, to_apply=%region_9.10 | all-reduce | flops 9216 | bytes 73728 | tf_op jit(solution)/shard_map/psum | solution.py:154
  596.8 8.1 %collective-permute-start.5 = (bf16[1024,2]{1,0:T(8,128)(2,1)S(1)}, bf16[1024,2]{1,0:T(8,128)(2,1)S(1)}, u32[]{:S(2)}, u32[]{:S(2)}) collective-permute-start(bf16[1024,2]{1,0:T(8,128)(2,1)S(1)} %slice.184), channel_id=1, source_target_pairs={{8,0},{16,8},{24,16},{32,24},{40,32},{48,40},{56,48},{64,56},{72,6... | collective-permute-start | bytes 12296 | tf_op jit(solution)/shard_map/ppermute | solution.py:14
  605.0 2.2 collective-permute-start.4
  607.2 7.1 %fusion.26 = bf16[1024,768]{1,0:T(8,128)(2,1)} fusion(bf16[1024,768]{1,0:T(8,128)(2,1)} %bitcast.133, bf16[1024,2]{1,0:T(8,128)(2,1)} %collective-permute-done.2, f32[1024]{0:T(1024)S(1)} %bitcast.159, f32[1024]{0:T(1024)S(1)} %bitcast.161, f32[1024]{0:T(1024)S(1)} %bitcast.157), kind=kLoop, calls=%fused_computation.60 | loop fusion | flops 11796480 | bytes 3162112 | tf_op jit(solution)/shard_map/convert_element_type | solution.py:66
  614.3 3.5 fusion.38
  617.8 3.5 fusion.32
  (39 shorter events, 0.2 us)
Async XLA Ops:
  0.6 10.2 %copy-start.5 = (bf16[1024,768]{1,0:T(8,128)(2,1)S(1)}, bf16[1024,768]{1,0:T(8,128)(2,1)}, u32[]{:S(2)}) copy-start(bf16[1024,768]{1,0:T(8,128)(2,1)} %param.9) | copy-start | bytes 4718596
  0.6 13.9 %copy-start.13 = (f32[3,3,1024]{2,1,0:T(4,128)S(1)}, f32[3,3,1024]{2,1,0:T(4,128)}, u32[]{:S(2)}) copy-start(f32[3,3,1024]{2,1,0:T(4,128)} %param.13) | copy-start | bytes 110596
  0.7 47.1 %all-to-all-start = ((bf16[32,32,768]{2,1,0:T(8,128)(2,1)}), bf16[32,32,768]{2,1,0:T(8,128)(2,1)S(1)}, u32[]{:S(2)}, u32[]{:S(2)}) async-start(bf16[32,32,768]{2,1,0:T(8,128)(2,1)} %bitcast.139), calls=%async_computation | async-start | bytes 3145728 | tf_op jit(solution)/shard_map/all_to_all | solution.py:129
  11.0 13.4 %collective-permute-start.3 = (bf16[1024,2]{1,0:T(8,128)(2,1)S(1)}, bf16[1024,2]{1,0:T(8,128)(2,1)S(1)}, u32[]{:S(2)}, u32[]{:S(2)}) collective-permute-start(bf16[1024,2]{1,0:T(8,128)(2,1)S(1)} %slice.154), channel_id=1, source_target_pairs={{0,8},{8,16},{16,24},{24,32},{32,40},{40,48},{48,56},{56,64},{64,7... | collective-permute-start | bytes 12296 | tf_op jit(solution)/shard_map/ppermute | solution.py:14
  24.3 0.7 copy-start.7
  47.7 31.9 %copy-start.1 = (bf16[32,32,768]{2,1,0:T(8,128)(2,1)}, bf16[32,32,768]{2,1,0:T(8,128)(2,1)S(1)}, u32[]{:S(2)}) copy-start(bf16[32,32,768]{2,1,0:T(8,128)(2,1)S(1)} %all-to-all-done) | copy-start | bytes 4718596
  47.7 48.4 %all-to-all-start.4 = ((bf16[32,32,768]{2,1,0:T(8,128)(2,1)}), bf16[32,32,768]{2,1,0:T(8,128)(2,1)S(1)}, u32[]{:S(2)}, u32[]{:S(2)}) async-start(bf16[32,32,768]{2,1,0:T(8,128)(2,1)} %bitcast.137), calls=%async_computation.4 | async-start | bytes 3145728 | tf_op jit(solution)/shard_map/all_to_all | solution.py:126
  60.3 12.4 %collective-permute-start = (bf16[1024,2]{1,0:T(8,128)(2,1)S(1)}, bf16[1024,2]{1,0:T(8,128)(2,1)S(1)}, u32[]{:S(2)}, u32[]{:S(2)}) collective-permute-start(bf16[1024,2]{1,0:T(8,128)(2,1)S(1)} %slice.138), channel_id=1, source_target_pairs={{0,8},{8,16},{16,24},{24,32},{32,40},{40,48},{48,56},{56,64},{64,7... | collective-permute-start | bytes 12296 | tf_op jit(solution)/shard_map/ppermute | solution.py:14
  72.7 0.7 copy-start.9
  96.1 35.2 %copy-start.3 = (bf16[32,32,768]{2,1,0:T(8,128)(2,1)}, bf16[32,32,768]{2,1,0:T(8,128)(2,1)S(1)}, u32[]{:S(2)}) copy-start(bf16[32,32,768]{2,1,0:T(8,128)(2,1)S(1)} %all-to-all-done.4) | copy-start | bytes 4718596
  96.1 51.6 %all-to-all-start.1 = ((bf16[32,32,768]{2,1,0:T(8,128)(2,1)}), bf16[32,32,768]{2,1,0:T(8,128)(2,1)S(1)}, u32[]{:S(2)}, u32[]{:S(2)}) async-start(bf16[32,32,768]{2,1,0:T(8,128)(2,1)} %bitcast.136), calls=%async_computation.1 | async-start | bytes 3145728 | tf_op jit(solution)/shard_map/all_to_all | solution.py:127
  111.9 12.4 %collective-permute-start.1 = (bf16[1024,2]{1,0:T(8,128)(2,1)S(1)}, bf16[1024,2]{1,0:T(8,128)(2,1)S(1)}, u32[]{:S(2)}, u32[]{:S(2)}) collective-permute-start(bf16[1024,2]{1,0:T(8,128)(2,1)S(1)} %slice.144), channel_id=1, source_target_pairs={{0,8},{8,16},{16,24},{24,32},{32,40},{40,48},{48,56},{56,64},{64,7... | collective-permute-start | bytes 12296 | tf_op jit(solution)/shard_map/ppermute | solution.py:14
  124.3 0.7 copy-start.10
  125.0 37.6 %copy-start.15 = (bf16[32]{0:T(256)(128)(2,1)S(1)}, bf16[32]{0:T(256)(128)(2,1)}, u32[]{:S(2)}) copy-start(bf16[32]{0:T(256)(128)(2,1)} %param.15) | copy-start | bytes 196
  125.0 37.6 %copy-start.14 = (bf16[2,128]{1,0:T(2,128)(2,1)S(1)}, bf16[2,128]{1,0:T(2,128)(2,1)}, u32[]{:S(2)}) copy-start(bf16[2,128]{1,0:T(2,128)(2,1)} %param.14) | copy-start | bytes 1540
  125.0 37.7 %copy-start.12 = (s32[32768]{0:T(1024)S(1)}, s32[32768]{0:T(1024)}, u32[]{:S(2)}) copy-start(s32[32768]{0:T(1024)} %constant.47) | copy-start | bytes 393220
  147.7 14.9 %copy-start.4 = (bf16[32,32,768]{2,1,0:T(8,128)(2,1)}, bf16[32,32,768]{2,1,0:T(8,128)(2,1)S(1)}, u32[]{:S(2)}) copy-start(bf16[32,32,768]{2,1,0:T(8,128)(2,1)S(1)} %all-to-all-done.1) | copy-start | bytes 4718596
  147.7 145.1 %all-to-all-start.2 = ((bf16[32,32,768]{2,1,0:T(8,128)(2,1)}), bf16[32,32,768]{2,1,0:T(8,128)(2,1)S(1)}, u32[]{:S(2)}, u32[]{:S(2)}) async-start(bf16[32,32,768]{2,1,0:T(8,128)(2,1)} %bitcast.135), calls=%async_computation.2 | async-start | bytes 3145728 | tf_op jit(solution)/shard_map/all_to_all | solution.py:128
  277.8 7.1 %copy-start.2 = (bf16[32,32,768]{2,1,0:T(8,128)(2,1)S(1)}, bf16[32,32,768]{2,1,0:T(8,128)(2,1)}, u32[]{:S(2)}) copy-start(bf16[32,32,768]{2,1,0:T(8,128)(2,1)} %copy-done.1) | copy-start | bytes 4718596
  294.8 6.0 copy-start.11
  375.8 41.1 %all-to-all-start.6 = ((bf16[32,32,768]{2,0,1:T(8,128)(2,1)}), bf16[32,32,768]{2,0,1:T(8,128)(2,1)S(1)}, u32[]{:S(2)}, u32[]{:S(2)}) async-start(bf16[32,32,768]{2,0,1:T(8,128)(2,1)} %get-tuple-element.19), calls=%async_computation.6 | async-start | bytes 3145728 | tf_op jit(solution)/shard_map/all_to_all | solution.py:144
  416.9 43.1 %all-to-all-start.5 = ((bf16[32,32,768]{2,0,1:T(8,128)(2,1)}), bf16[32,32,768]{2,0,1:T(8,128)(2,1)S(1)}, u32[]{:S(2)}, u32[]{:S(2)}) async-start(bf16[32,32,768]{2,0,1:T(8,128)(2,1)} %fusion.19), calls=%async_computation.5 | async-start | bytes 3145728 | tf_op jit(solution)/shard_map/all_to_all | solution.py:143
  430.9 15.0 %copy-start.8 = (bf16[1024,2]{1,0:T(8,128)(2,1)S(1)}, bf16[1024,2]{1,0:T(8,128)(2,1)}, u32[]{:S(2)}) copy-start(bf16[1024,2]{1,0:T(8,128)(2,1)} %copy-done.7) | copy-start | bytes 12292
  435.3 10.6 %copy-start = (bf16[32,32,768]{2,0,1:T(8,128)(2,1)S(1)}, bf16[32,32,768]{2,0,1:T(8,128)(2,1)}, u32[]{:S(2)}) copy-start(bf16[32,32,768]{2,0,1:T(8,128)(2,1)} %all_to_all.100) | copy-start | bytes 4718596
  435.3 10.6 %copy-start.6 = (bf16[1024,768]{1,0:T(8,128)(2,1)S(1)}, bf16[1024,768]{1,0:T(8,128)(2,1)}, u32[]{:S(2)}) copy-start(bf16[1024,768]{1,0:T(8,128)(2,1)} %param.9) | copy-start | bytes 4718596
  437.9 169.3 %collective-permute-start.2 = (bf16[1024,2]{1,0:T(8,128)(2,1)}, bf16[1024,2]{1,0:T(8,128)(2,1)}, u32[]{:S(2)}, u32[]{:S(2)}) collective-permute-start(bf16[1024,2]{1,0:T(8,128)(2,1)} %slice.174), channel_id=1, source_target_pairs={{8,0},{16,8},{24,16},{32,24},{40,32},{48,40},{56,48},{64,56},{72,6... | collective-permute-start | bytes 12296 | tf_op jit(solution)/shard_map/ppermute | solution.py:14
  596.8 17.4 %collective-permute-start.5 = (bf16[1024,2]{1,0:T(8,128)(2,1)S(1)}, bf16[1024,2]{1,0:T(8,128)(2,1)S(1)}, u32[]{:S(2)}, u32[]{:S(2)}) collective-permute-start(bf16[1024,2]{1,0:T(8,128)(2,1)S(1)} %slice.184), channel_id=1, source_target_pairs={{8,0},{16,8},{24,16},{32,24},{40,32},{48,40},{56,48},{64,56},{72,6... | collective-permute-start | bytes 12296 | tf_op jit(solution)/shard_map/ppermute | solution.py:14
  605.0 12.8 %collective-permute-start.4 = (bf16[1024,2]{1,0:T(8,128)(2,1)S(1)}, bf16[1024,2]{1,0:T(8,128)(2,1)S(1)}, u32[]{:S(2)}, u32[]{:S(2)}) collective-permute-start(bf16[1024,2]{1,0:T(8,128)(2,1)S(1)} %slice.181), channel_id=1, source_target_pairs={{8,0},{16,8},{24,16},{32,24},{40,32},{48,40},{56,48},{64,56},{72,6... | collective-permute-start | bytes 12296 | tf_op jit(solution)/shard_map/ppermute | solution.py:14
where the time goes:
time: 623 us; the launch traced here: 621 us
  blocking collectives  178 us (29%)
  local copies, waits for them, and re-layouts  157 us (25%)
  waiting for transfers between devices  126 us (20%)
  starting transfers between devices  84.7 us (14%)
  other arithmetic  63.7 us (10%)
  matrix products  11.4 us (2%)
    psum x1, blocking collectives, body(): grad_short = lax.psum(jnp.stack([tap_query, tap_key, tap_value]), 'ctx')  131 us
    gather x2, local copies, waits for them, and re-layouts, toeplitz(): picked = jnp.take(filt, np.clip(offset, 0, TAPS - 1).reshape(-1), axis=1)  122 us
    all_to_all x1, blocking collectives, body(): lax.all_to_all(grad_qgrp, 'ctx', split_axis=1, concat_axis=0, tiled=True)  46.5 us
    all_to_all x1, waiting for transfers between devices, body(): lax.all_to_all(grad_vgrp, 'ctx', split_axis=1, concat_axis=0, tiled=True)  33.8 us
    ppermute x6, waiting for transfers between devices, shifted(): return lax.ppermute(block, axis, route)  27.5 us
    ppermute x6, starting transfers between devices, shifted(): return lax.ppermute(block, axis, route)  23.1 us
    all_to_all x1, waiting for transfers between devices, body(): lax.all_to_all(grad_out, 'ctx', split_axis=0, concat_axis=1, tiled=True)  19.7 us
    all_to_all x1, waiting for transfers between devices, body(): lax.all_to_all(query_conv, 'ctx', split_axis=0, concat_axis=1, tiled=True)  16.5 us
  transfers between devices with their start and end apart: 12, of which 8 were waited for; matrix products, arithmetic and copies ran while one was open for 31% of the time, Pallas kernels for 0%

commit v1 on v0

v1 whole, which is shorter than its diff:
```python
import functools

import jax
import jax.numpy as jnp
from jax import lax
from jax.experimental import pallas as pl
from jax.experimental.pallas import tpu as pltpu
from jax.sharding import PartitionSpec as P

TAPS = 128
SHORT = 3
GROUP = 16
LANE = 128
TILE = 128
CHUNKS = 4
BF = jnp.bfloat16
F32 = jnp.float32
MESH = pl.DeviceIdType.MESH


def nn(a, b):
    return lax.dot_general(a, b, (((1,), (0,)), ((), ())), preferred_element_type=F32)


def nt(a, b):
    return lax.dot_general(a, b, (((1,), (1,)), ((), ())), preferred_element_type=F32)


def tn(a, b):
    return lax.dot_general(a, b, (((0,), (0,)), ((), ())), preferred_element_type=F32)


def iota(shape, axis):
    return lax.broadcasted_iota(jnp.int32, shape, axis)


def kernel(
    n, blocks,
    q_hbm, k_hbm, v_hbm, g_hbm, taps, fmsg,
    out_q, out_k, out_v, out_short, out_filt, out_bias,
    qx, kx, vx, gx, kc, vc, pr, gm, gw, acc, ph, gh, taps_b, bias_b,
    rim_s, rim_r, filt_s, filt_r, msg_s, msg_r, tot_s, tot_r, edge_s, edge_r,
    in_sem, rim_sem, ph_ssem, ph_rsem, gh_ssem, gh_rsem, filt_sem, msg_sem, tot_sem, edge_sem,
):
    me = lax.axis_index("ctx")
    channels = qx.shape[0]
    tiles = channels // TILE
    last = blocks - 1
    width = blocks * LANE
    chunks = min(CHUNKS, tiles)
    part = channels // chunks
    right, left = lax.rem(me + 1, n), lax.rem(me + n - 1, n)
    has_left, has_right = me > 0, me < n - 1
    tail = (blocks - 2) * LANE

    def piece(i, src, dst, start, size):
        cols = pl.ds(start, size)
        return pltpu.make_async_copy(src.at[:, cols], dst.at[:, cols], in_sem.at[i])

    loads = [
        piece(0, k_hbm, kx, tail, 2 * LANE),
        piece(1, v_hbm, vx, tail, 2 * LANE),
        piece(2, q_hbm, qx, tail, 2 * LANE),
        piece(3, k_hbm, kx, 0, tail),
        piece(4, v_hbm, vx, 0, tail),
        piece(5, q_hbm, qx, 0, tail),
        piece(6, g_hbm, gx, 0, width),
    ]
    for load in loads:
        load.start()

    barrier = pltpu.get_barrier_semaphore()

    def greet(d, carry):
        pl.semaphore_signal(
            barrier, inc=1, device_id={"ctx": lax.rem(me + d, n)}, device_id_type=MESH
        )
        return carry

    lax.fori_loop(1, n, greet, 0)

    lane16 = iota((GROUP, LANE), 1)
    first1, first2 = lane16 < 1, lane16 < 2
    last1, last2 = lane16 >= LANE - 1, lane16 >= LANE - 2
    zero16 = jnp.zeros((GROUP, LANE), BF)
    eye = iota((TILE, TILE), 0) == iota((TILE, TILE), 1)
    ones = jnp.ones((TILE, LANE), BF)

    def spread(row):
        return nn(jnp.where(eye, row, 0.0).astype(BF), ones).astype(BF)

    def tap_tile(t, carry):
        cols = pl.ds(pl.multiple_of(t * TILE, TILE), TILE)
        for w in range(3):
            for j in range(SHORT):
                taps_b[w * 3 + j, cols, :] = spread(taps[w, j : j + 1, cols])
        return carry

    lax.fori_loop(0, tiles, tap_tile, 0)

    own = fmsg[...]
    own_bias = pltpu.roll(own[2:3, :], lax.rem(me, 4) * 32, 1)
    filt_s[...] = jnp.concatenate([own[0:2], own_bias, jnp.zeros((5, LANE), F32)], axis=0)
    filt_r[me] = filt_s[...]

    sub8, lane8 = iota((8, LANE), 0), iota((8, LANE), 1)

    def pick(w, first_lane):
        return ((sub8 // 2 == w) & (lane8 == first_lane + sub8 % 2)).astype(F32).astype(BF)

    loads[0].wait()
    loads[1].wait()
    loads[2].wait()
    final = pl.ds(last * LANE, LANE)
    rim_s[...] = (
        nt(pick(0, LANE - 2), qx[:, final])
        + nt(pick(1, LANE - 2), kx[:, final])
        + nt(pick(2, LANE - 2), vx[:, final])
    )

    def shift_right(cur, prev, by, mask):
        before = zero16 if prev is None else pltpu.roll(prev, by, 1)
        return jnp.where(mask, before, pltpu.roll(cur, by, 1))

    def short_forward(w, rows, cur, prev):
        return (
            taps_b[w * 3, rows, :] * cur
            + taps_b[w * 3 + 1, rows, :] * shift_right(cur, prev, 1, first1)
            + taps_b[w * 3 + 2, rows, :] * shift_right(cur, prev, 2, first2)
        )

    def lanes(i):
        return pl.ds(i * LANE, LANE)

    def tail_rows(t, carry):
        for u in range(4):
            rows = pl.ds(pl.multiple_of(t * 64 + u * GROUP, GROUP), GROUP)
            kv = []
            for w, (src, dst) in ((1, (kx, kc)), (2, (vx, vc))):
                y = short_forward(w, rows, src[rows, lanes(last)], src[rows, lanes(last - 1)])
                dst[rows, lanes(last)] = y
                kv.append(y)
            pr[rows, lanes(last)] = kv[0] * kv[1]
        return carry

    lax.fori_loop(0, channels // 64, tail_rows, 0)

    pl.semaphore_wait(barrier, n - 1)

    rim_copy = pltpu.make_async_remote_copy(
        src_ref=rim_s, dst_ref=rim_r, send_sem=rim_sem.at[0], recv_sem=rim_sem.at[1],
        device_id={"ctx": right}, device_id_type=MESH,
    )

    def ph_copy(c):
        rows = pl.ds(c * part, part)
        return pltpu.make_async_remote_copy(
            src_ref=pr.at[rows, lanes(last)], dst_ref=ph.at[rows, :],
            send_sem=ph_ssem.at[c], recv_sem=ph_rsem.at[c],
            device_id={"ctx": right}, device_id_type=MESH,
        )

    def gh_copy(c):
        rows = pl.ds(c * part, part)
        return pltpu.make_async_remote_copy(
            src_ref=gm.at[rows, lanes(0)], dst_ref=gh.at[rows, :],
            send_sem=gh_ssem.at[c], recv_sem=gh_rsem.at[c],
            device_id={"ctx": left}, device_id_type=MESH,
        )

    @pl.when(has_right)
    def _():
        rim_copy.start()
        ph_copy(0).start()

    def filt_copy(d):
        return pltpu.make_async_remote_copy(
            src_ref=filt_s, dst_ref=filt_r.at[me], send_sem=filt_sem.at[0], recv_sem=filt_sem.at[1],
            device_id={"ctx": lax.rem(me + d, n)}, device_id_type=MESH,
        )

    def send_filt(d, carry):
        filt_copy(d).start()
        return carry

    lax.fori_loop(1, n, send_filt, 0)

    @pl.when(has_right)
    def _():
        for c in range(1, chunks):
            ph_copy(c).start()

    for load in loads[3:]:
        load.wait()

    def forward_rows(t, carry):
        for u in range(4):
            rows = pl.ds(pl.multiple_of(t * 64 + u * GROUP, GROUP), GROUP)
            for i in range(blocks):
                before = lambda src: None if i == 0 else src[rows, lanes(i - 1)]
                if i < last:
                    kk = short_forward(1, rows, kx[rows, lanes(i)], before(kx))
                    vv = short_forward(2, rows, vx[rows, lanes(i)], before(vx))
                    kc[rows, lanes(i)] = kk
                    vc[rows, lanes(i)] = vv
                    pr[rows, lanes(i)] = kk * vv
                qq = short_forward(0, rows, qx[rows, lanes(i)], before(qx))
                gm[rows, lanes(i)] = gx[rows, lanes(i)] * qq
        return carry

    lax.fori_loop(0, channels // 64, forward_rows, 0)

    @pl.when(has_left)
    def _():
        rim_copy.wait_recv()

    @pl.when(jnp.logical_not(has_left))
    def _():
        rim_r[...] = jnp.zeros(rim_r.shape, F32)
        ph[...] = jnp.zeros(ph.shape, BF)

    @pl.when(jnp.logical_not(has_right))
    def _():
        edge_r[...] = jnp.zeros(edge_r.shape, F32)
        gh[...] = jnp.zeros(gh.shape, BF)

    sub16, wide = iota((16, 3 * LANE), 0), iota((16, 3 * LANE), 1)

    def place(first_lane):
        hit = (sub16 // 2 == wide // LANE) & (wide % LANE == first_lane + sub16 % 2)
        return (hit & (sub16 < 6)).astype(F32).astype(BF)

    def head_tile(t, carry):
        cols = pl.ds(pl.multiple_of(t * TILE, TILE), TILE)
        x = rim_r[:, cols]
        rows = []
        for w in range(3):
            tap1, tap2 = taps[w, 1:2, cols], taps[w, 2:3, cols]
            x2, x1 = x[2 * w : 2 * w + 1], x[2 * w + 1 : 2 * w + 2]
            rows += [tap1 * x1 + tap2 * x2, tap2 * x1]
        rows.append(jnp.zeros((10, TILE), F32))
        fix = tn(jnp.concatenate(rows, axis=0).astype(BF), place(0)).astype(BF)
        kk = kc[cols, lanes(0)] + fix[:, LANE : 2 * LANE]
        vv = vc[cols, lanes(0)] + fix[:, 2 * LANE :]
        kc[cols, lanes(0)] = kk
        vc[cols, lanes(0)] = vv
        pr[cols, lanes(0)] = kk * vv
        gm[cols, lanes(0)] = gm[cols, lanes(0)] + gx[cols, lanes(0)] * fix[:, :LANE]
        return carry

    lax.fori_loop(0, tiles, head_tile, 0)

    @pl.when(has_left)
    def _():
        for c in range(chunks):
            gh_copy(c).start()

    def drain(ref, sem):
        pltpu.make_async_copy(ref, ref, sem).wait()

    others = pl.ds(0, n - 1)
    drain(filt_r.at[others], filt_sem.at[1])

    def bias_tile(t, carry):
        row = (
            filt_r[t * 4, 2:3, :] + filt_r[t * 4 + 1, 2:3, :]
            + filt_r[t * 4 + 2, 2:3, :] + filt_r[t * 4 + 3, 2:3, :]
        )
        bias_b[pl.ds(pl.multiple_of(t * TILE, TILE), TILE), :] = spread(row)
        return carry

    lax.fori_loop(0, tiles, bias_tile, 0)

    sq_row, sq_col = iota((LANE, LANE), 0), iota((LANE, LANE), 1)
    upper = sq_col >= sq_row
    late = sq_col + sq_row >= LANE - 1
    flip = (sq_col + sq_row == LANE - 1).astype(F32).astype(BF)
    zero_sq = jnp.zeros((LANE, LANE), BF)
    ones8 = jnp.ones((8, LANE), BF)

    def shift_left(cur, nxt, by, mask):
        after = zero16 if nxt is None else pltpu.roll(nxt, LANE - by, 1)
        return jnp.where(mask, after, pltpu.roll(cur, LANE - by, 1))

    def msg_copy(o):
        return pltpu.make_async_remote_copy(
            src_ref=msg_s.at[o], dst_ref=msg_r.at[me], send_sem=msg_sem.at[0], recv_sem=msg_sem.at[1],
            device_id={"ctx": o}, device_id_type=MESH,
        )

    def main_tile(t, carry):
        base = t * TILE

        for c in range(chunks):
            @pl.when(base == c * part)
            def _():
                @pl.when(has_left)
                def _():
                    ph_copy(c).wait_recv()

                @pl.when(has_right)
                def _():
                    gh_copy(c).wait_recv()

        for u in range(TILE // GROUP):
            rows = pl.ds(pl.multiple_of(base + u * GROUP, GROUP), GROUP)
            own_rows = pl.ds(u * GROUP, GROUP)
            slot = t * 4 + u // 2
            filt = filt_r[slot, u % 2 : u % 2 + 1, :].astype(BF)
            round_filt = pltpu.roll(
                jnp.broadcast_to(filt, (LANE, LANE)), 0, 1, stride=1, stride_axis=0
            )
            now = jnp.where(upper, round_filt, zero_sq)
            then = jnp.where(upper, zero_sq, round_filt)
            p = [pr[rows, lanes(i)] for i in range(blocks)]
            m = [gm[rows, lanes(i)] for i in range(blocks)]
            p_ext = jnp.concatenate([ph[rows, :]] + p, axis=0)
            m_all = jnp.concatenate(m, axis=0)
            m_next = jnp.concatenate(m[1:] + [gh[rows, :]], axis=0)
            depth = blocks * GROUP
            mixed = nn(
                jnp.concatenate([p_ext[:depth], p_ext[GROUP:]], axis=1),
                jnp.concatenate([then, now], axis=0),
            ).astype(BF)
            back = nt(
                jnp.concatenate([m_all, m_next], axis=1),
                jnp.concatenate([now, then], axis=1),
            ).astype(BF)
            p_turned = nt(flip, p_ext).astype(BF)
            pad = jnp.zeros((GROUP, LANE), BF)
            m_pair = jnp.concatenate(
                [jnp.concatenate([m_all, pad], axis=0), jnp.concatenate([pad, m_all], axis=0)], axis=1
            )
            diff = nn(p_turned, m_pair)
            diff = jnp.where(late, diff[:, LANE:], diff[:, :LANE])
            diff = pltpu.roll(diff, 1, 1, stride=1, stride_axis=0)
            msg_s[slot, u % 2 : u % 2 + 1, :] = jnp.sum(diff, axis=0, keepdims=True)

            bias = bias_b[rows, :]
            bias_sum = None
            for i in range(blocks):
                block = pl.ds(i * GROUP, GROUP)
                mixed_i = mixed[i * GROUP : (i + 1) * GROUP] + bias * p[i]
                back_i = back[i * GROUP : (i + 1) * GROUP] + bias * m[i]
                gw[0, own_rows, lanes(i)] = gx[rows, lanes(i)] * mixed_i
                gw[1, own_rows, lanes(i)] = back_i * vc[rows, lanes(i)]
                gw[2, own_rows, lanes(i)] = back_i * kc[rows, lanes(i)]
                term = m[i] * p[i]
                bias_sum = term if bias_sum is None else bias_sum + term
            acc[9, own_rows, :] = bias_sum

            for w, (src, dst) in enumerate(((qx, out_q), (kx, out_k), (vx, out_v))):
                sums = [None] * SHORT
                tap = [taps_b[w * 3 + j, rows, :] for j in range(SHORT)]
                for i in range(blocks):
                    g0 = gw[w, own_rows, lanes(i)]
                    nxt = None if i == last else gw[w, own_rows, lanes(i + 1)]
                    shifted = [g0, shift_left(g0, nxt, 1, last1), shift_left(g0, nxt, 2, last2)]
                    dst[rows, lanes(i)] = tap[0] * shifted[0] + tap[1] * shifted[1] + tap[2] * shifted[2]
                    x = src[rows, lanes(i)]
                    for j in range(SHORT):
                        term = shifted[j] * x
                        sums[j] = term if sums[j] is None else sums[j] + term
                for j in range(SHORT):
                    acc[w * 3 + j, own_rows, :] = sums[j]

        cols = pl.ds(pl.multiple_of(base, TILE), TILE)
        edge = (
            nt(pick(0, 0), gw[0, :, 0:LANE])
            + nt(pick(1, 0), gw[1, :, 0:LANE])
            + nt(pick(2, 0), gw[2, :, 0:LANE])
        )
        edge_s[:, cols] = edge
        x = rim_r[:, cols]
        bias_row = nt(ones8, acc[9])[0:1]
        for w in range(3):
            g0, g1 = edge[2 * w : 2 * w + 1], edge[2 * w + 1 : 2 * w + 2]
            x2, x1 = x[2 * w : 2 * w + 1], x[2 * w + 1 : 2 * w + 2]
            row0 = nt(ones8, acc[w * 3])[0:1]
            row1 = nt(ones8, acc[w * 3 + 1])[0:1] + g0 * x1
            row2 = nt(ones8, acc[w * 3 + 2])[0:1] + g0 * x2 + g1 * x1
            msg_s[t * 4 + w, 2:6, :] = jnp.concatenate([bias_row, row0, row1, row2], axis=0)
        msg_s[t * 4 + 3, 2:6, :] = jnp.concatenate(
            [bias_row, jnp.zeros((3, LANE), F32)], axis=0
        )
        for i in range(4):
            o = t * 4 + i

            @pl.when(o != me)
            def _():
                msg_copy(o).start()

        return carry

    def clear(o, carry):
        msg_s[o] = jnp.zeros((8, LANE), F32)
        return carry

    lax.fori_loop(0, n, clear, 0)
    lax.fori_loop(0, tiles, main_tile, 0)

    edge_copy = pltpu.make_async_remote_copy(
        src_ref=edge_s, dst_ref=edge_r, send_sem=edge_sem.at[0], recv_sem=edge_sem.at[1],
        device_id={"ctx": left}, device_id_type=MESH,
    )

    @pl.when(has_left)
    def _():
        edge_copy.start()

    msg_r[me] = msg_s[me]
    drain(msg_r.at[others], msg_sem.at[1])

    def add_up(o, total):
        return total + msg_r[o]

    total = lax.fori_loop(0, n, add_up, jnp.zeros((8, LANE), F32), unroll=8)
    out_filt[...] = total[0:2]
    out_bias[...] = pltpu.roll(total[2:3], lax.rem(LANE - lax.rem(me, 4) * 32, LANE), 1)
    tot_s[...] = jnp.concatenate([total[3:6], jnp.zeros((5, LANE), F32)], axis=0)
    tot_r[me] = tot_s[...]

    def tot_copy(d):
        return pltpu.make_async_remote_copy(
            src_ref=tot_s, dst_ref=tot_r.at[me], send_sem=tot_sem.at[0], recv_sem=tot_sem.at[1],
            device_id={"ctx": lax.rem(me + d, n)}, device_id_type=MESH,
        )

    def send_tot(d, carry):
        tot_copy(d).start()
        return carry

    lax.fori_loop(1, n, send_tot, 0)

    @pl.when(has_right)
    def _():
        edge_copy.wait_recv()

    def end_tile(t, carry):
        cols = pl.ds(pl.multiple_of(t * TILE, TILE), TILE)
        x = edge_r[:, cols]
        rows = []
        for w in range(3):
            tap1, tap2 = taps[w, 1:2, cols], taps[w, 2:3, cols]
            g0, g1 = x[2 * w : 2 * w + 1], x[2 * w + 1 : 2 * w + 2]
            rows += [tap2 * g0, tap1 * g0 + tap2 * g1]
        rows.append(jnp.zeros((10, TILE), F32))
        fix = tn(jnp.concatenate(rows, axis=0).astype(BF), place(LANE - 2)).astype(BF)
        for w, dst in enumerate((out_q, out_k, out_v)):
            dst[cols, lanes(last)] = dst[cols, lanes(last)] + fix[:, w * LANE : (w + 1) * LANE]
        return carry

    lax.fori_loop(0, tiles, end_tile, 0)

    drain(tot_r.at[others], tot_sem.at[1])
    for w in range(3):
        for t in range(tiles):
            out_short[w, :, t * TILE : (t + 1) * TILE] = tot_r[t * 4 + w, 0:SHORT, :]

    drain(filt_r.at[others], filt_sem.at[0])
    drain(msg_r.at[others], msg_sem.at[0])
    drain(tot_r.at[others], tot_sem.at[0])

    @pl.when(has_right)
    def _():
        rim_copy.wait_send()
        for c in range(chunks):
            ph_copy(c).wait_send()

    @pl.when(has_left)
    def _():
        edge_copy.wait_send()
        for c in range(chunks):
            gh_copy(c).wait_send()


def body(query_feat, key_feat, value_feat, grad_out, short_taps, filters, skip_bias):
    channels, length = query_feat.shape
    n = lax.axis_size("ctx")
    blocks = length // LANE
    bias_row = jnp.pad(skip_bias.astype(F32), (0, LANE - skip_bias.shape[0]))[None, :]
    fmsg = jnp.concatenate([filters.astype(F32), bias_row, jnp.zeros((5, LANE), F32)], axis=0)
    full = (channels, length)
    vmem = pl.BlockSpec(memory_space=pltpu.VMEM)
    hbm = pl.BlockSpec(memory_space=pl.ANY)
    outs = pl.pallas_call(
        functools.partial(kernel, n, blocks),
        out_shape=(
            pltpu.VMEM(full, BF), pltpu.VMEM(full, BF), pltpu.VMEM(full, BF),
            jax.ShapeDtypeStruct((3, SHORT, channels), F32),
            jax.ShapeDtypeStruct((2, LANE), F32),
            jax.ShapeDtypeStruct((1, LANE), F32),
        ),
        in_specs=[hbm] * 4 + [vmem] * 2,
        out_specs=(vmem,) * 6,
        scratch_shapes=[
            pltpu.VMEM(full, BF), pltpu.VMEM(full, BF), pltpu.VMEM(full, BF), pltpu.VMEM(full, BF),
            pltpu.VMEM(full, BF), pltpu.VMEM(full, BF), pltpu.VMEM(full, BF), pltpu.VMEM(full, BF),
            pltpu.VMEM((3, TILE, length), BF),
            pltpu.VMEM((10, TILE, LANE), BF),
            pltpu.VMEM((channels, LANE), BF), pltpu.VMEM((channels, LANE), BF),
            pltpu.VMEM((9, channels, LANE), BF),
            pltpu.VMEM((channels, LANE), BF),
            pltpu.VMEM((8, channels), F32), pltpu.VMEM((8, channels), F32),
            pltpu.VMEM((8, LANE), F32), pltpu.VMEM((n, 8, LANE), F32),
            pltpu.VMEM((n, 8, LANE), F32), pltpu.VMEM((n, 8, LANE), F32),
            pltpu.VMEM((8, LANE), F32), pltpu.VMEM((n, 8, LANE), F32),
            pltpu.VMEM((8, channels), F32), pltpu.VMEM((8, channels), F32),
            pltpu.SemaphoreType.DMA((7,)),
            pltpu.SemaphoreType.DMA((2,)),
            pltpu.SemaphoreType.DMA((CHUNKS,)), pltpu.SemaphoreType.DMA((CHUNKS,)),
            pltpu.SemaphoreType.DMA((CHUNKS,)), pltpu.SemaphoreType.DMA((CHUNKS,)),
            pltpu.SemaphoreType.DMA((2,)),
            pltpu.SemaphoreType.DMA((2,)),
            pltpu.SemaphoreType.DMA((2,)),
            pltpu.SemaphoreType.DMA((2,)),
        ],
        compiler_params=pltpu.CompilerParams(
            collective_id=0, has_side_effects=True, vmem_limit_bytes=48 * 1024 * 1024
        ),
    )(query_feat, key_feat, value_feat, grad_out, short_taps, fmsg)
    grad_query, grad_key, grad_value, grad_short, grad_filters, bias_out = outs
    return (
        grad_query, grad_key, grad_value, grad_short, grad_filters,
        bias_out[0, : skip_bias.shape[0]],
    )


def solution(mesh):
    in_specs = (
        P("tp", "ctx"),
        P("tp", "ctx"),
        P("tp", "ctx"),
        P("tp", "ctx"),
        P(None, None, "tp"),
        P(("tp", "ctx"), None),
        P(("tp", "ctx")),
    )
    out_specs = (
        P("tp", "ctx"),
        P("tp", "ctx"),
        P("tp", "ctx"),
        P(None, None, "tp"),
        P(("tp", "ctx"), None),
        P(("tp", "ctx")),
    )
    return jax.shard_map(body, mesh=mesh, in_specs=in_specs, out_specs=out_specs, check_vma=False)
```

time: 623 us -> 48 us (0.08)
  blocking collectives: 178 us -> 0 us
  local copies, waits for them, and re-layouts: 157 us -> 6 us
  waiting for transfers between devices: 126 us -> 0 us
  starting transfers between devices: 84.7 us -> 0 us
  other arithmetic: 63.7 us -> 1.39 us
  Pallas kernels: 0 us -> 39.8 us
  matrix products: 11.4 us -> 0 us
    psum x1 -> x0, blocking collectives: 131 us -> none  [body(): grad_short = lax.psum(jnp.stack([tap_query, tap_key, tap_value]), 'ctx')]
    gather x2 -> x0, local copies, waits for them, and re-layouts: 122 us -> none  [toeplitz(): picked = jnp.take(filt, np.clip(offset, 0, TAPS - 1).reshape(-1), axis=1)]
    all_to_all x6 -> x0, waiting for transfers between devices: 98.1 us -> none  [the longest x1 33.8 us: body(): lax.all_to_all(grad_vgrp, 'ctx', split_axis=1, concat_axis=0, tiled=True)]
    all_to_all x6 -> x0, starting transfers between devices: 61.6 us -> none  [the longest x1 14.9 us: body(): lax.all_to_all(value_conv, 'ctx', split_axis=0, concat_axis=1, tiled=True)]
    all_to_all x1 -> x0, blocking collectives: 46.5 us -> none  [body(): lax.all_to_all(grad_qgrp, 'ctx', split_axis=1, concat_axis=0, tiled=True)]
    pallas_call x0 -> x1, Pallas kernels: none -> 39.8 us  [body(): pl.pallas_call(functools.partial(kernel, n, blocks), out_shape=(pltpu.VME...]
    convert_element_type x10 -> x1, other arithmetic: 36.5 us -> 0.66 us  [body(): filters.astype(F32)]
    ppermute x6 -> x0, waiting for transfers between devices: 27.5 us -> none  [shifted(): return lax.ppermute(block, axis, route)]
  transfers between devices with their start and end apart: 12 -> 0, of which waited for: 8 -> 0; matrix products, arithmetic and copies ran while one was open for 31% -> 0% of each run, Pallas kernels for 0% -> 0%
where the time goes in v1:
time: 48 us; the launch traced here: 47.9 us
  Pallas kernels  39.8 us (83%)
  local copies, waits for them, and re-layouts  6 us (12%)
  other arithmetic  1.39 us (3%)
  between operations  0.65 us (1%)
    pallas_call x1, Pallas kernels, body(): pl.pallas_call(functools.partial(kernel, n, blocks), out_shape=(pltpu.VME...  39.8 us
    unnamed x7, local copies, waits for them, and re-layouts  5.41 us

profile of v1, /device:TPU:1, one launch (start us, length us, event | category | flops | bytes accessed | tf_op | source)
XLA Modules:
  0.0 47.9 jit_solution(8197344096866126789)
XLA Ops:
  0.6 0.7 %bitcast_convert_fusion = f32[1,128]{1,0:T(1,128)S(1)} fusion(bf16[32]{0:T(256)(128)(2,1)} %param.13), kind=kLoop, calls=%fused_computation.1 | loop fusion | flops 128 | bytes 576 | tf_op jit(solution)/shard_map/broadcast_in_dim | solution.py:481
  1.3 0.1 pad.8.clone
  1.4 0.7 %convert_element_type.6 = f32[2,128]{1,0:T(2,128)S(1)} convert(bf16[2,128]{1,0:T(2,128)(2,1)} %param.12) | non-fusion elementwise | flops 256 | bytes 1536 | tf_op jit(solution)/shard_map/convert_element_type | solution.py:482
  2.0 0.1 maximum_maximum_fusion.fmsg
  2.1 0.0 copy-start
  2.1 0.8 %copy-done = f32[3,3,1024]{2,1,0:T(4,128)S(1)} copy-done((f32[3,3,1024]{2,1,0:T(4,128)S(1)}, f32[3,3,1024]{2,1,0:T(4,128)}, u32[]{:S(2)}) %copy-start) | copy-done | bytes 36888
  2.9 39.8 %shard_map.118 = (bf16[1024,768]{1,0:T(8,128)(2,1)S(1)}, bf16[1024,768]{1,0:T(8,128)(2,1)S(1)}, bf16[1024,768]{1,0:T(8,128)(2,1)S(1)}, f32[3,3,1024]{2,1,0:T(4,1...) custom-call(bf16[1024,768]{1,0:T(8,128)(2,1)} %q_hbm.1, bf16[1024,768]{1,0:T(8,128)(2,1)} %k_hbm.1, ...), custom_call_target="tpu_custom_call" | custom-call | tf_op jit(solution)/shard_map/pallas_call | solution.py:486
  42.7 1.1 %copy.18 = bf16[1024,768]{1,0:T(8,128)(2,1)} copy(bf16[1024,768]{1,0:T(8,128)(2,1)S(1)} %get-tuple-element.18) | data formatting | bytes 3145728
  43.9 0.5 %slice_bitcast_fusion = f32[32]{0:T(128)} fusion(f32[1,128]{1,0:T(1,128)S(1)} %get-tuple-element.17), kind=kLoop, calls=%fused_computation.2 | loop fusion | bytes 256 | tf_op jit(solution)/shard_map/squeeze | solution.py:525
  44.4 1.1 %copy.19 = bf16[1024,768]{1,0:T(8,128)(2,1)} copy(bf16[1024,768]{1,0:T(8,128)(2,1)S(1)} %get-tuple-element.19) | data formatting | bytes 3145728
  45.5 1.1 %copy.20 = bf16[1024,768]{1,0:T(8,128)(2,1)} copy(bf16[1024,768]{1,0:T(8,128)(2,1)S(1)} %get-tuple-element.20) | data formatting | bytes 3145728
  46.7 0.6 %copy.21 = f32[3,3,1024]{2,1,0:T(4,128)} copy(f32[3,3,1024]{2,1,0:T(4,128)S(1)} %get-tuple-element.33) | data formatting | bytes 73728
  47.3 0.6 %copy.22 = f32[2,128]{1,0:T(2,128)} copy(f32[2,128]{1,0:T(2,128)S(1)} %get-tuple-element.34) | data formatting | bytes 2048
  (1 shorter events, 0.0 us)
Async XLA Ops:
  2.1 0.8 %copy-start = (f32[3,3,1024]{2,1,0:T(4,128)S(1)}, f32[3,3,1024]{2,1,0:T(4,128)}, u32[]{:S(2)}) copy-start(f32[3,3,1024]{2,1,0:T(4,128)} %taps.1) | copy-start | bytes 110596

commit v2 on v1

v2 whole, which is shorter than its diff:
```python
import functools

import jax
import jax.numpy as jnp
from jax import lax
from jax.experimental import pallas as pl
from jax.experimental.pallas import tpu as pltpu
from jax.sharding import PartitionSpec as P

TAPS = 128
SHORT = 3
GROUP = 16
LANE = 128
TILE = 128
CHUNKS = 4
BF = jnp.bfloat16
F32 = jnp.float32
MESH = pl.DeviceIdType.MESH


def nn(a, b):
    return lax.dot_general(a, b, (((1,), (0,)), ((), ())), preferred_element_type=F32)


def nt(a, b):
    return lax.dot_general(a, b, (((1,), (1,)), ((), ())), preferred_element_type=F32)


def tn(a, b):
    return lax.dot_general(a, b, (((0,), (0,)), ((), ())), preferred_element_type=F32)


def iota(shape, axis):
    return lax.broadcasted_iota(jnp.int32, shape, axis)


def lanes(i):
    return pl.ds(i * LANE, LANE)


def place(firsts):
    sub, lane = iota((16, LANE), 0), iota((16, LANE), 1)
    blocks = [
        ((sub // 2 == w) & (lane == first + sub % 2)).astype(F32).astype(BF)
        for w, first in enumerate(firsts)
    ]
    return jnp.concatenate(blocks, axis=1)


def kernel(
    n, blocks,
    q_hbm, k_hbm, v_hbm, g_hbm, taps_hbm, filt_hbm, bias_hbm,
    out_q, out_k, out_v, out_edge, out_short, out_filt, out_bias,
    qx, kx, vx, gx, kc, vc, pr, gm, gmr, conv, acc, heads, first, after, ph, gh, taps, filt_in, bias_in, taps_b, bias_b,
    rim_s, rim_r, col_s, col_r, filt_s, filt_r, msg_s, msg_r, tot_s, tot_r, edge_s, edge_r,
    in_sem, rim_sem, col_sem, ph_ssem, ph_rsem, gh_ssem, gh_rsem, filt_sem, msg_sem, tot_sem, edge_sem,
):
    me = lax.axis_index("ctx")
    channels = qx.shape[0]
    tiles = channels // TILE
    chunks = min(CHUNKS, tiles)
    last = blocks - 1
    part = channels // chunks
    right, left = lax.rem(me + 1, n), lax.rem(me + n - 1, n)
    has_left, has_right = me > 0, me < n - 1

    def piece(i, src, dst, start, size):
        cols = pl.ds(start * LANE, size * LANE)
        return pltpu.make_async_copy(src.at[:, cols], dst.at[:, cols], in_sem.at[i])

    loads = [
        pltpu.make_async_copy(taps_hbm, taps, in_sem.at[0]),
        pltpu.make_async_copy(filt_hbm, filt_in, in_sem.at[1]),
        pltpu.make_async_copy(bias_hbm, bias_in, in_sem.at[2]),
        piece(3, k_hbm, kx, blocks - 2, 2),
        piece(4, v_hbm, vx, blocks - 2, 2),
        piece(5, q_hbm, qx, last, 1),
        piece(6, q_hbm, qx, 0, 1),
        piece(7, g_hbm, gx, 0, 1),
        piece(8, k_hbm, kx, 0, blocks - 2),
        piece(9, v_hbm, vx, 0, blocks - 2),
        piece(10, q_hbm, qx, 1, blocks - 2),
        piece(11, g_hbm, gx, 1, blocks - 1),
    ]
    for load in loads:
        load.start()

    barrier = pltpu.get_barrier_semaphore()

    def greet(d, carry):
        pl.semaphore_signal(
            barrier, inc=1, device_id={"ctx": lax.rem(me + d, n)}, device_id_type=MESH
        )
        return carry

    lax.fori_loop(1, n, greet, 0)

    lane16 = iota((GROUP, LANE), 1)
    first1, first2 = lane16 < 1, lane16 < 2
    last1, last2 = lane16 >= LANE - 1, lane16 >= LANE - 2
    zero16 = jnp.zeros((GROUP, LANE), BF)
    eye = iota((TILE, TILE), 0) == iota((TILE, TILE), 1)
    ones = jnp.ones((TILE, LANE), BF)
    flip = (iota((LANE, LANE), 0) + iota((LANE, LANE), 1) == LANE - 1).astype(F32).astype(BF)

    def spread(row):
        return nn(jnp.where(eye, row, 0.0).astype(BF), ones).astype(BF)

    loads[0].wait()

    def tap_tile(t, carry):
        cols = pl.ds(pl.multiple_of(t * TILE, TILE), TILE)
        for w in range(3):
            for j in range(SHORT):
                taps_b[w * 3 + j, cols, :] = spread(taps[w, j : j + 1, cols])
        return carry

    lax.fori_loop(0, tiles, tap_tile, 0)

    loads[1].wait()
    loads[2].wait()
    own_bias = bias_in[...].astype(F32).reshape(1, -1)
    own_bias = jnp.pad(own_bias, ((0, 0), (0, LANE - own_bias.shape[1])))
    own_bias = pltpu.roll(own_bias, lax.rem(me, 4) * 32, 1)
    filt_s[...] = jnp.concatenate(
        [filt_in[...].astype(F32), own_bias, jnp.zeros((5, LANE), F32)], axis=0
    )
    filt_r[me] = filt_s[...]

    sub8, lane8 = iota((8, LANE), 0), iota((8, LANE), 1)

    def pick(w, first_lane):
        return ((sub8 // 2 == w) & (lane8 == first_lane + sub8 % 2)).astype(F32).astype(BF)

    def shift_right(cur, before, mask):
        return jnp.where(mask, zero16 if before is None else before, cur)

    def short_forward(tap, x, r1, r2, b1, b2):
        return tap[0] * x + tap[1] * shift_right(r1, b1, first1) + tap[2] * shift_right(r2, b2, first2)

    for load in loads[3:8]:
        load.wait()
    rim_s[...] = (
        nt(pick(0, LANE - 2), qx[:, lanes(last)])
        + nt(pick(1, LANE - 2), kx[:, lanes(last)])
        + nt(pick(2, LANE - 2), vx[:, lanes(last)])
    )
    col_s[...] = nt(pick(0, 0), gx[:, lanes(0)])

    def tap_of(w, rows):
        return [taps_b[w * 3 + j, rows, :] for j in range(SHORT)]

    def border_rows(t, carry):
        for u in range(4):
            rows = pl.ds(pl.multiple_of(t * 64 + u * GROUP, GROUP), GROUP)
            kv = []
            for w, (src, dst) in ((1, (kx, kc)), (2, (vx, vc))):
                x, prev = src[rows, lanes(last)], src[rows, lanes(last - 1)]
                y = short_forward(
                    tap_of(w, rows), x, pltpu.roll(x, 1, 1), pltpu.roll(x, 2, 1),
                    pltpu.roll(prev, 1, 1), pltpu.roll(prev, 2, 1),
                )
                dst[rows, lanes(last)] = y
                kv.append(y)
            pr[rows, lanes(last)] = kv[0] * kv[1]
            x = qx[rows, lanes(0)]
            y = short_forward(tap_of(0, rows), x, pltpu.roll(x, 1, 1), pltpu.roll(x, 2, 1), None, None)
            gm[rows, lanes(0)] = gx[rows, lanes(0)] * y
        return carry

    lax.fori_loop(0, channels // 64, border_rows, 0)

    pl.semaphore_wait(barrier, n - 1)

    rim_copy = pltpu.make_async_remote_copy(
        src_ref=rim_s, dst_ref=rim_r, send_sem=rim_sem.at[0], recv_sem=rim_sem.at[1],
        device_id={"ctx": right}, device_id_type=MESH,
    )
    col_copy = pltpu.make_async_remote_copy(
        src_ref=col_s, dst_ref=col_r, send_sem=col_sem.at[0], recv_sem=col_sem.at[1],
        device_id={"ctx": left}, device_id_type=MESH,
    )

    def ph_copy(c):
        rows = pl.ds(c * part, part)
        return pltpu.make_async_remote_copy(
            src_ref=pr.at[rows, lanes(last)], dst_ref=ph.at[rows, :],
            send_sem=ph_ssem.at[c], recv_sem=ph_rsem.at[c],
            device_id={"ctx": right}, device_id_type=MESH,
        )

    def gh_copy(c):
        rows = pl.ds(c * part, part)
        return pltpu.make_async_remote_copy(
            src_ref=gm.at[rows, lanes(0)], dst_ref=gh.at[rows, :],
            send_sem=gh_ssem.at[c], recv_sem=gh_rsem.at[c],
            device_id={"ctx": left}, device_id_type=MESH,
        )

    @pl.when(has_right)
    def _():
        rim_copy.start()
        ph_copy(0).start()

    @pl.when(has_left)
    def _():
        col_copy.start()
        gh_copy(0).start()

    def filt_copy(d):
        return pltpu.make_async_remote_copy(
            src_ref=filt_s, dst_ref=filt_r.at[me], send_sem=filt_sem.at[0], recv_sem=filt_sem.at[1],
            device_id={"ctx": lax.rem(me + d, n)}, device_id_type=MESH,
        )

    def send_filt(d, carry):
        filt_copy(d).start()
        return carry

    lax.fori_loop(1, n, send_filt, 0)

    @pl.when(has_right)
    def _():
        for c in range(1, chunks):
            ph_copy(c).start()

    @pl.when(has_left)
    def _():
        for c in range(1, chunks):
            gh_copy(c).start()

    for load in loads[8:]:
        load.wait()

    def forward_rows(t, carry):
        turned = []
        for u in range(4):
            rows = pl.ds(pl.multiple_of(t * 64 + u * GROUP, GROUP), GROUP)
            taps3 = [tap_of(w, rows) for w in range(3)]
            b1, b2 = [None] * 3, [None] * 3
            for i in range(blocks):
                short = [None] * 3
                for w, src in enumerate((qx, kx, vx)):
                    if i == last and w > 0:
                        continue
                    x = src[rows, lanes(i)]
                    r1, r2 = pltpu.roll(x, 1, 1), pltpu.roll(x, 2, 1)
                    if i > 0 or w > 0:
                        short[w] = short_forward(taps3[w], x, r1, r2, b1[w], b2[w])
                    b1[w], b2[w] = r1, r2
                if i < last:
                    kc[rows, lanes(i)] = short[1]
                    vc[rows, lanes(i)] = short[2]
                    pr[rows, lanes(i)] = short[1] * short[2]
                if i > 0:
                    m = gx[rows, lanes(i)] * short[0]
                    gm[rows, lanes(i)] = m
                    turned.append(m)
        turned = nn(jnp.concatenate(turned, axis=0), flip).astype(BF)
        for u in range(4):
            rows = pl.ds(pl.multiple_of(t * 64 + u * GROUP, GROUP), GROUP)
            for i in range(1, blocks):
                at = (u * last + i - 1) * GROUP
                gmr[rows, lanes(i)] = turned[at : at + GROUP]
        return carry

    lax.fori_loop(0, channels // 64, forward_rows, 0)

    @pl.when(has_left)
    def _():
        rim_copy.wait_recv()

    @pl.when(jnp.logical_not(has_left))
    def _():
        rim_r[...] = jnp.zeros(rim_r.shape, F32)
        ph[...] = jnp.zeros(ph.shape, BF)

    @pl.when(has_right)
    def _():
        col_copy.wait_recv()

    @pl.when(jnp.logical_not(has_right))
    def _():
        col_r[...] = jnp.zeros(col_r.shape, F32)
        edge_r[...] = jnp.zeros(edge_r.shape, F32)
        gh[...] = jnp.zeros(gh.shape, BF)

    def drain(ref, sem):
        pltpu.make_async_copy(ref, ref, sem).wait()

    others = pl.ds(0, n - 1)
    drain(filt_r.at[others], filt_sem.at[1])

    sq_row, sq_col = iota((LANE, LANE), 0), iota((LANE, LANE), 1)
    upper = sq_col >= sq_row
    early = sq_col + sq_row <= LANE - 1
    zero_sq = jnp.zeros((LANE, LANE), BF)
    rim_place = place((0, 0, 0, 0))
    pad = jnp.zeros((GROUP, LANE), BF)

    def shift_left(cur, after, mask):
        return jnp.where(mask, zero16 if after is None else after, cur)

    def msg_copy(o):
        return pltpu.make_async_remote_copy(
            src_ref=msg_s.at[o], dst_ref=msg_r.at[me], send_sem=msg_sem.at[0], recv_sem=msg_sem.at[1],
            device_id={"ctx": o}, device_id_type=MESH,
        )

    def halo_ready(base):
        for c in range(chunks):
            @pl.when(base == c * part)
            def _():
                @pl.when(has_left)
                def _():
                    ph_copy(c).wait_recv()

                @pl.when(has_right)
                def _():
                    gh_copy(c).wait_recv()

    def rims_in(t):
        cols = pl.ds(pl.multiple_of(t * TILE, TILE), TILE)
        rim, own, far = rim_r[:, cols], rim_s[:, cols], col_r[:, cols]
        rows = []
        for w in range(3):
            tap1, tap2 = taps[w, 1:2, cols], taps[w, 2:3, cols]
            x2, x1 = rim[2 * w : 2 * w + 1], rim[2 * w + 1 : 2 * w + 2]
            rows += [tap1 * x1 + tap2 * x2, tap2 * x1]
        tap1, tap2 = taps[0, 1:2, cols], taps[0, 2:3, cols]
        rows += [far[0:1] * (tap1 * own[1:2] + tap2 * own[0:1]), far[1:2] * (tap2 * own[1:2])]
        rows.append(jnp.zeros((8, TILE), F32))
        fix = tn(jnp.concatenate(rows, axis=0).astype(BF), rim_place).astype(BF)
        kk = kc[cols, lanes(0)] + fix[:, LANE : 2 * LANE]
        vv = vc[cols, lanes(0)] + fix[:, 2 * LANE : 3 * LANE]
        kc[cols, lanes(0)] = kk
        vc[cols, lanes(0)] = vv
        pr[cols, lanes(0)] = kk * vv
        m0 = gm[cols, lanes(0)] + gx[cols, lanes(0)] * fix[:, :LANE]
        first[cols, :] = m0
        gmr[cols, lanes(0)] = nn(m0, flip).astype(BF)
        after[cols, :] = gh[cols, :] + fix[:, 3 * LANE :]
        bias_b[cols, :] = spread(
            filt_r[t * 4, 2:3, :] + filt_r[t * 4 + 1, 2:3, :]
            + filt_r[t * 4 + 2, 2:3, :] + filt_r[t * 4 + 3, 2:3, :]
        )

    depth = blocks * GROUP

    def matmuls(t, u):
        rows = pl.ds(pl.multiple_of(t * TILE + u * GROUP, GROUP), GROUP)
        slot = t * 4 + u // 2
        filt = filt_r[slot, u % 2 : u % 2 + 1, :].astype(BF)
        round_filt = pltpu.roll(jnp.broadcast_to(filt, (LANE, LANE)), 0, 1, stride=1, stride_axis=0)
        now = jnp.where(upper, round_filt, zero_sq)
        then = jnp.where(upper, zero_sq, round_filt)
        p = [ph[rows, :]] + [pr[rows, lanes(i)] for i in range(blocks)]
        m = [first[rows, :]] + [gm[rows, lanes(i)] for i in range(1, blocks)] + [after[rows, :]]
        p_ext = jnp.concatenate(p, axis=0)
        m_ext = jnp.concatenate(m, axis=0)
        conv[u % 2, 0] = nn(
            jnp.concatenate([p_ext[:depth], p_ext[GROUP:]], axis=1),
            jnp.concatenate([then, now], axis=0),
        ).astype(BF)
        conv[u % 2, 1] = nt(
            jnp.concatenate([m_ext[:depth], m_ext[GROUP:]], axis=1),
            jnp.concatenate([now, then], axis=1),
        ).astype(BF)
        m_rev = [gmr[rows, lanes(i)] for i in range(blocks)]
        diff = tn(
            p_ext,
            jnp.concatenate(
                [jnp.concatenate(m_rev + [pad], axis=0), jnp.concatenate([pad] + m_rev, axis=0)], axis=1
            ),
        )
        diff = jnp.where(early, diff[:, LANE:], diff[:, :LANE]).astype(BF)
        diff = pltpu.roll(diff, 0, 1, stride=1, stride_axis=0)
        msg_s[slot, u % 2 : u % 2 + 1, :] = jnp.sum(diff.astype(F32), axis=0, keepdims=True)

    def gradients(t, u):
        rows = pl.ds(pl.multiple_of(t * TILE + u * GROUP, GROUP), GROUP)
        own_rows = pl.ds(u * GROUP, GROUP)
        bias = bias_b[rows, :]
        bias_sum = None
        gw = [[None] * blocks for _ in range(3)]
        for i in range(blocks):
            p = pr[rows, lanes(i)]
            m = first[rows, :] if i == 0 else gm[rows, lanes(i)]
            mixed = conv[u % 2, 0, pl.ds(i * GROUP, GROUP), :] + bias * p
            back = conv[u % 2, 1, pl.ds(i * GROUP, GROUP), :] + bias * m
            gw[0][i] = gx[rows, lanes(i)] * mixed
            gw[1][i] = back * vc[rows, lanes(i)]
            gw[2][i] = back * kc[rows, lanes(i)]
            term = m * p
            bias_sum = term if bias_sum is None else bias_sum + term
        acc[lax.rem(t, 2), 9, own_rows, :] = bias_sum
        for w, (src, dst) in enumerate(((qx, out_q), (kx, out_k), (vx, out_v))):
            sums = [None] * SHORT
            tap = tap_of(w, rows)
            a1 = a2 = None
            for i in reversed(range(blocks)):
                g0 = gw[w][i]
                r1, r2 = pltpu.roll(g0, LANE - 1, 1), pltpu.roll(g0, LANE - 2, 1)
                shifted = [g0, shift_left(r1, a1, last1), shift_left(r2, a2, last2)]
                a1, a2 = r1, r2
                dst[rows, lanes(i)] = tap[0] * shifted[0] + tap[1] * shifted[1] + tap[2] * shifted[2]
                x = src[rows, lanes(i)]
                for j in range(SHORT):
                    term = shifted[j] * x
                    sums[j] = term if sums[j] is None else sums[j] + term
            for j in range(SHORT):
                acc[lax.rem(t, 2), w * 3 + j, own_rows, :] = sums[j]
            heads[lax.rem(t, 2), w, own_rows, :] = gw[w][0]

    halves = ((iota((8, 2 * LANE), 1) // LANE) == iota((8, 2 * LANE), 0)).astype(F32).astype(BF)

    def lane_sums(a, b, c, d):
        sums = nt(
            halves,
            jnp.concatenate(
                [jnp.concatenate([a, b], axis=1), jnp.concatenate([c, d], axis=1)], axis=0
            ),
        )
        return [sums[0:1, :LANE], sums[1:2, :LANE], sums[0:1, LANE:], sums[1:2, LANE:]]

    def tile_sums(t):
        cols = pl.ds(pl.multiple_of(t * TILE, TILE), TILE)
        k = lax.rem(t, 2)
        edge = (
            nt(pick(0, 0), heads[k, 0]) + nt(pick(1, 0), heads[k, 1]) + nt(pick(2, 0), heads[k, 2])
        )
        edge_s[:, cols] = edge
        rim = rim_r[:, cols]
        sums = lane_sums(acc[k, 0], acc[k, 1], acc[k, 2], acc[k, 3])
        sums += lane_sums(acc[k, 4], acc[k, 5], acc[k, 6], acc[k, 7])
        sums += lane_sums(acc[k, 8], acc[k, 9], acc[k, 8], acc[k, 9])
        blank = jnp.zeros((2, LANE), F32)
        for w in range(3):
            g0, g1 = edge[2 * w : 2 * w + 1], edge[2 * w + 1 : 2 * w + 2]
            x2, x1 = rim[2 * w : 2 * w + 1], rim[2 * w + 1 : 2 * w + 2]
            row1 = sums[w * 3 + 1] + g0 * x1
            row2 = sums[w * 3 + 2] + g0 * x2 + g1 * x1
            msg_s[t * 4 + w, 2:8, :] = jnp.concatenate([sums[9], sums[w * 3], row1, row2, blank], axis=0)
        msg_s[t * 4 + 3, 2:8, :] = jnp.concatenate([sums[9], blank, blank, blank[:1]], axis=0)

    def send_sums(t):
        for i in range(4):
            o = t * 4 + i

            @pl.when(o != me)
            def _():
                msg_copy(o).start()

    def main_tile(t, before, ahead):
        if ahead:
            halo_ready((t + 1) * TILE)
        steps = TILE // GROUP
        matmuls(t, 0)
        if before:
            tile_sums(t - 1)
        for u in range(steps):
            if u + 1 < steps:
                matmuls(t, u + 1)
            if ahead and u == 2:
                rims_in(t + 1)
            gradients(t, u)
        if before:
            send_sums(t - 1)

    def middle_tile(t, carry):
        main_tile(t, True, True)
        return carry

    halo_ready(0)
    rims_in(0)
    main_tile(0, False, True)
    lax.fori_loop(1, tiles - 1, middle_tile, 0)
    main_tile(tiles - 1, True, False)
    tile_sums(tiles - 1)
    send_sums(tiles - 1)

    edge_copy = pltpu.make_async_remote_copy(
        src_ref=edge_s, dst_ref=edge_r, send_sem=edge_sem.at[0], recv_sem=edge_sem.at[1],
        device_id={"ctx": left}, device_id_type=MESH,
    )

    @pl.when(has_left)
    def _():
        edge_copy.start()

    msg_r[me] = msg_s[me]
    drain(msg_r.at[others], msg_sem.at[1])

    total = msg_r[0]
    for o in range(1, n):
        total = total + msg_r[o]
    tot_s[...] = jnp.concatenate([total[3:6], jnp.zeros((5, LANE), F32)], axis=0)

    def tot_copy(d):
        return pltpu.make_async_remote_copy(
            src_ref=tot_s, dst_ref=tot_r.at[me], send_sem=tot_sem.at[0], recv_sem=tot_sem.at[1],
            device_id={"ctx": lax.rem(me + d, n)}, device_id_type=MESH,
        )

    def send_tot(d, carry):
        tot_copy(d).start()
        return carry

    lax.fori_loop(1, n, send_tot, 0)
    tot_r[me] = tot_s[...]
    out_filt[...] = lax.dot_general(
        total, flip.astype(F32), (((1,), (0,)), ((), ())),
        preferred_element_type=F32, precision=lax.Precision.HIGHEST,
    )[0:2]
    out_bias[...] = pltpu.roll(total[2:3], lax.rem(LANE - lax.rem(me, 4) * 32, LANE), 1)

    @pl.when(has_right)
    def _():
        edge_copy.wait_recv()

    out_edge[...] = edge_r[...]

    drain(filt_r.at[others], filt_sem.at[0])
    drain(msg_r.at[others], msg_sem.at[0])

    @pl.when(has_right)
    def _():
        rim_copy.wait_send()
        for c in range(chunks):
            ph_copy(c).wait_send()

    @pl.when(has_left)
    def _():
        col_copy.wait_send()
        edge_copy.wait_send()
        for c in range(chunks):
            gh_copy(c).wait_send()

    drain(tot_r.at[others], tot_sem.at[1])
    for w in range(3):
        for t in range(tiles):
            out_short[w, :, t * TILE : (t + 1) * TILE] = tot_r[t * 4 + w, 0:SHORT, :]
    drain(tot_r.at[others], tot_sem.at[0])


def finish(
    blocks,
    gq, gk, gv, edge, short, filt, bias, taps_hbm,
    out_q, out_k, out_v, out_short, out_filt, out_bias,
    taps, ends, bias_v, sem, end_sem,
):
    last = blocks - 1
    bulk = pl.ds(0, last * LANE)
    copies = [pltpu.make_async_copy(taps_hbm, taps, sem.at[0])]
    for i, (src, dst) in enumerate(((gq, out_q), (gk, out_k), (gv, out_v))):
        copies.append(pltpu.make_async_copy(src.at[:, bulk], dst.at[:, bulk], sem.at[1 + i]))
    copies.append(pltpu.make_async_copy(short, out_short, sem.at[4]))
    copies.append(pltpu.make_async_copy(filt, out_filt, sem.at[5]))
    for copy in copies:
        copy.start()
    bias_v[...] = bias[0, : bias_v.shape[0]]
    copies.append(pltpu.make_async_copy(bias_v, out_bias, sem.at[6]))
    copies[-1].start()
    copies[0].wait()
    rim_place = place((LANE - 2, LANE - 2, LANE - 2))
    for t in range(gq.shape[0] // TILE):
        cols = pl.ds(t * TILE, TILE)
        x = edge[:, cols]
        rows = []
        for w in range(3):
            tap1, tap2 = taps[w, 1:2, cols], taps[w, 2:3, cols]
            g0, g1 = x[2 * w : 2 * w + 1], x[2 * w + 1 : 2 * w + 2]
            rows += [tap2 * g0, tap1 * g0 + tap2 * g1]
        rows.append(jnp.zeros((10, TILE), F32))
        fix = tn(jnp.concatenate(rows, axis=0).astype(BF), rim_place).astype(BF)
        for w, src in enumerate((gq, gk, gv)):
            ends[w, cols, :] = src[cols, lanes(last)] + fix[:, w * LANE : (w + 1) * LANE]
    for w, dst in enumerate((out_q, out_k, out_v)):
        copies.append(pltpu.make_async_copy(ends.at[w], dst.at[:, lanes(last)], end_sem.at[w]))
        copies[-1].start()
    for copy in copies[1:]:
        copy.wait()


def body(query_feat, key_feat, value_feat, grad_out, short_taps, filters, skip_bias):
    channels, length = query_feat.shape
    n = lax.axis_size("ctx")
    blocks = length // LANE
    full, tile = (channels, length), (channels, LANE)
    vmem = pl.BlockSpec(memory_space=pltpu.VMEM)
    hbm = pl.BlockSpec(memory_space=pltpu.HBM)
    dma = pltpu.SemaphoreType.DMA
    row = pltpu.VMEM((8, channels), F32)
    slots = pltpu.VMEM((n, 8, LANE), F32)
    one = pltpu.VMEM((8, LANE), F32)
    outs = pl.pallas_call(
        functools.partial(kernel, n, blocks),
        out_shape=(
            pltpu.VMEM(full, BF), pltpu.VMEM(full, BF), pltpu.VMEM(full, BF),
            row,
            pltpu.VMEM(short_taps.shape, F32),
            pltpu.VMEM(filters.shape, F32),
            pltpu.VMEM((1, LANE), F32),
        ),
        in_specs=[hbm] * 7,
        out_specs=(vmem,) * 7,
        scratch_shapes=[pltpu.VMEM(full, BF)] * 9
        + [
            pltpu.VMEM((2, 2, blocks * GROUP, LANE), BF),
            pltpu.VMEM((2, 10, TILE, LANE), BF),
            pltpu.VMEM((2, 3, TILE, LANE), BF),
            pltpu.VMEM(tile, BF), pltpu.VMEM(tile, BF),
            pltpu.VMEM(tile, BF), pltpu.VMEM(tile, BF),
            pltpu.VMEM(short_taps.shape, F32),
            pltpu.VMEM(filters.shape, BF),
            pltpu.VMEM(skip_bias.shape, BF),
            pltpu.VMEM((9, channels, LANE), BF),
            pltpu.VMEM(tile, BF),
            row, row, row, row, one, slots, slots, slots, one, slots, row, row,
            dma((12,)), dma((2,)), dma((2,)),
            dma((CHUNKS,)), dma((CHUNKS,)), dma((CHUNKS,)), dma((CHUNKS,)),
            dma((2,)), dma((2,)), dma((2,)), dma((2,)),
        ],
        compiler_params=pltpu.CompilerParams(
            collective_id=0, has_side_effects=True, vmem_limit_bytes=48 * 1024 * 1024
        ),
    )(query_feat, key_feat, value_feat, grad_out, short_taps, filters, skip_bias)
    return pl.pallas_call(
        functools.partial(finish, blocks),
        out_shape=tuple(
            jax.ShapeDtypeStruct(s, d)
            for s, d in (
                (full, BF), (full, BF), (full, BF),
                (short_taps.shape, F32), (filters.shape, F32), (skip_bias.shape, F32),
            )
        ),
        in_specs=[vmem] * 7 + [hbm],
        out_specs=(hbm,) * 6,
        scratch_shapes=[
            pltpu.VMEM(short_taps.shape, F32),
            pltpu.VMEM((3,) + tile, BF),
            pltpu.VMEM(skip_bias.shape, F32),
            dma((7,)), dma((3,)),
        ],
        compiler_params=pltpu.CompilerParams(vmem_limit_bytes=16 * 1024 * 1024),
    )(*outs, short_taps)


def solution(mesh):
    wide, narrow = P("tp", "ctx"), P(None, None, "tp")
    both = ("tp", "ctx")

    def whole(*args):
        with jax.sharding.use_abstract_mesh(mesh.abstract_mesh):
            return jax.shard_map(
                body,
                mesh=mesh,
                in_specs=(wide, wide, wide, wide, narrow, P(both, None), P(both)),
                out_specs=(wide, wide, wide, narrow, P(both, None), P(both)),
                check_vma=False,
            )(*args)

    return whole
```

time: 48 us -> 42 us (0.88)
  local copies, waits for them, and re-layouts: 6 us -> 2.1 us
  other arithmetic: 1.39 us -> 0 us
  Pallas kernels: 39.8 us -> 39 us
    unnamed x7 -> x6, local copies, waits for them, and re-layouts: 5.41 us -> 2.1 us
    pallas_call x1, Pallas kernels: 39.8 us -> 36.7 us  [body(): pl.pallas_call(functools.partial(kernel, n, blocks), out_shape=(pltpu.VME...]
    pallas_call x0 -> x1, Pallas kernels: none -> 2.34 us  [body(): pl.pallas_call(functools.partial(finish, blocks), out_shape=tuple((jax.Sh...]
    broadcast_in_dim x1 -> x0, other arithmetic: 0.66 us -> none  [body(): jnp.pad(skip_bias.astype(F32), (0, LANE - skip_bias.shape[0]))[None, :]]
    convert_element_type x1 -> x0, other arithmetic: 0.66 us -> none  [body(): filters.astype(F32)]
    squeeze x1 -> x0, local copies, waits for them, and re-layouts: 0.51 us -> none  [body(): bias_out[0, :skip_bias.shape[0]]]
where the time goes in v2:
time: 42 us; the launch traced here: 41.8 us
  Pallas kernels  39 us (93%)
  local copies, waits for them, and re-layouts  2.1 us (5%)
  between operations  0.65 us (2%)
    pallas_call x1, Pallas kernels, body(): pl.pallas_call(functools.partial(kernel, n, blocks), out_shape=(pltpu.VME...  36.7 us
    pallas_call x1, Pallas kernels, body(): pl.pallas_call(functools.partial(finish, blocks), out_shape=tuple((jax.Sh...  2.34 us
    unnamed x6, local copies, waits for them, and re-layouts  2.1 us

profile of v2, /device:TPU:1, one launch (start us, length us, event | category | flops | bytes accessed | tf_op | source)
XLA Modules:
  0.0 41.8 jit_solution(9277360401038910269)
XLA Ops:
  0.6 0.0 copy-start
  0.6 0.8 %copy-done = f32[3,3,1024]{2,1,0:T(4,128)S(1)} copy-done((f32[3,3,1024]{2,1,0:T(4,128)S(1)}, f32[3,3,1024]{2,1,0:T(4,128)}, u32[]{:S(2)}) %copy-start) | copy-done | bytes 36888
  1.4 0.0 copy-start.1
  1.4 0.7 %copy-done.1 = bf16[2,128]{1,0:T(2,128)(2,1)S(1)} copy-done((bf16[2,128]{1,0:T(2,128)(2,1)S(1)}, bf16[2,128]{1,0:T(2,128)(2,1)}, u32[]{:S(2)}) %copy-start.1) | copy-done | bytes 536
  2.1 0.0 copy-start.2
  2.1 0.7 %copy-done.2 = bf16[32]{0:T(256)(128)(2,1)S(1)} copy-done((bf16[32]{0:T(256)(128)(2,1)S(1)}, bf16[32]{0:T(256)(128)(2,1)}, u32[]{:S(2)}) %copy-start.2) | copy-done | bytes 88
  2.7 36.7 %shard_map.118 = (bf16[1024,768]{1,0:T(8,128)(2,1)S(1)}, bf16[1024,768]{1,0:T(8,128)(2,1)S(1)}, bf16[1024,768]{1,0:T(8,128)(2,1)S(1)}, f32[8,1024]{1,0:T(8,128)S...) custom-call(bf16[1024,768]{1,0:T(8,128)(2,1)} %q_hbm.1, bf16[1024,768]{1,0:T(8,128)(2,1)} %k_hbm.1, ...), custom_call_target="tpu_custom_call" | custom-call | tf_op jit(solution)/shard_map/pallas_call | solution.py:596
  39.5 2.3 %shard_map.119 = (bf16[1024,768]{1,0:T(8,128)(2,1)}, bf16[1024,768]{1,0:T(8,128)(2,1)}, bf16[1024,768]{1,0:T(8,128)(2,1)}, f32[3,3,1024]{2,1,0:T(4,128)}, f32[2,128]{1,0:T(2,128)}, /*index=5*/f32[32]{0:T(128)}) custom-call(bf16[1024,768]{1,0:T(8,128)(2,1)S(1)} %get-tuple-element.13.gq, bf16[1024,768]{1,0:T(8,128)(2,1)S(1)} %get-tuple-element.14.gk, ...), custom_call_target="tpu_custom_call" | custom-call | tf_op jit(solution)/shard_map/pallas_call | solution.py:628
Async XLA Ops:
  0.6 0.8 %copy-start = (f32[3,3,1024]{2,1,0:T(4,128)S(1)}, f32[3,3,1024]{2,1,0:T(4,128)}, u32[]{:S(2)}) copy-start(f32[3,3,1024]{2,1,0:T(4,128)} %taps_hbm.3) | copy-start | bytes 110596
  1.4 0.7 %copy-start.1 = (bf16[2,128]{1,0:T(2,128)(2,1)S(1)}, bf16[2,128]{1,0:T(2,128)(2,1)}, u32[]{:S(2)}) copy-start(bf16[2,128]{1,0:T(2,128)(2,1)} %filt_hbm.1) | copy-start | bytes 1540
  2.1 0.7 %copy-start.2 = (bf16[32]{0:T(256)(128)(2,1)S(1)}, bf16[32]{0:T(256)(128)(2,1)}, u32[]{:S(2)}) copy-start(bf16[32]{0:T(256)(128)(2,1)} %bias_hbm.1) | copy-start | bytes 196

commit v3 on v2

--- a/solution.py
+++ b/solution.py
@@ -51,7 +51,7 @@
     n, blocks,
     q_hbm, k_hbm, v_hbm, g_hbm, taps_hbm, filt_hbm, bias_hbm,
     out_q, out_k, out_v, out_edge, out_short, out_filt, out_bias,
-    qx, kx, vx, gx, kc, vc, pr, gm, gmr, conv, acc, heads, first, after, ph, gh, taps, filt_in, bias_in, taps_b, bias_b,
+    qx, kx, vx, gx, kc, vc, pr, gm, gmr, raw, xs, conv, acc, heads, first, after, ph, gh, taps, filt_in, bias_in, taps_b, bias_b,
     rim_s, rim_r, col_s, col_r, filt_s, filt_r, msg_s, msg_r, tot_s, tot_r, edge_s, edge_r,
     in_sem, rim_sem, col_sem, ph_ssem, ph_rsem, gh_ssem, gh_rsem, filt_sem, msg_sem, tot_sem, edge_sem,
 ):
@@ -63,6 +63,15 @@
     part = channels // chunks
     right, left = lax.rem(me + 1, n), lax.rem(me + n - 1, n)
     has_left, has_right = me > 0, me < n - 1
+
+    def peer(k):
+        if n != 32:
+            return lax.rem(me + 1 + k, n)
+        i, j = k // 8, k // 2 % 4
+        dz = 1 + 2 * i - 3 * (i // 2)
+        dx = 2 - j + 3 * (j // 2) + 2 * (j // 3)
+        z, x, c = (me // 8 + dz) % 4, (me // 2 + dx) % 4, (me + 1 + k % 2) % 2
+        return z * 8 + x * 2 + c
 
     def piece(i, src, dst, start, size):
         cols = pl.ds(start * LANE, size * LANE)
@@ -106,16 +115,14 @@
     def spread(row):
         return nn(jnp.where(eye, row, 0.0).astype(BF), ones).astype(BF)
 
-    loads[0].wait()
-
-    def tap_tile(t, carry):
+    def tap_tile(t):
         cols = pl.ds(pl.multiple_of(t * TILE, TILE), TILE)
         for w in range(3):
             for j in range(SHORT):
                 taps_b[w * 3 + j, cols, :] = spread(taps[w, j : j + 1, cols])
-        return carry
-
-    lax.fori_loop(0, tiles, tap_tile, 0)
+
+    loads[0].wait()
+    tap_tile(0)
 
     loads[1].wait()
     loads[2].wait()
@@ -135,8 +142,11 @@
     def shift_right(cur, before, mask):
         return jnp.where(mask, zero16 if before is None else before, cur)
 
-    def short_forward(tap, x, r1, r2, b1, b2):
-        return tap[0] * x + tap[1] * shift_right(r1, b1, first1) + tap[2] * shift_right(r2, b2, first2)
+    def short_forward(w, rows, i, tap, x, r1, r2, b1, b2):
+        s1, s2 = shift_right(r1, b1, first1), shift_right(r2, b2, first2)
+        xs[w, 0, rows, lanes(i)] = s1
+        xs[w, 1, rows, lanes(i)] = s2
+        return tap[0] * x + tap[1] * s1 + tap[2] * s2
 
     for load in loads[3:8]:
         load.wait()
@@ -150,25 +160,32 @@
     def tap_of(w, rows):
         return [taps_b[w * 3 + j, rows, :] for j in range(SHORT)]
 
-    def border_rows(t, carry):
-        for u in range(4):
-            rows = pl.ds(pl.multiple_of(t * 64 + u * GROUP, GROUP), GROUP)
+    def border_tile(t):
+        for u in range(TILE // GROUP):
+            rows = pl.ds(pl.multiple_of(t * TILE + u * GROUP, GROUP), GROUP)
             kv = []
             for w, (src, dst) in ((1, (kx, kc)), (2, (vx, vc))):
                 x, prev = src[rows, lanes(last)], src[rows, lanes(last - 1)]
                 y = short_forward(
-                    tap_of(w, rows), x, pltpu.roll(x, 1, 1), pltpu.roll(x, 2, 1),
+                    w, rows, last, tap_of(w, rows), x, pltpu.roll(x, 1, 1), pltpu.roll(x, 2, 1),
                     pltpu.roll(prev, 1, 1), pltpu.roll(prev, 2, 1),
                 )
                 dst[rows, lanes(last)] = y
                 kv.append(y)
             pr[rows, lanes(last)] = kv[0] * kv[1]
             x = qx[rows, lanes(0)]
-            y = short_forward(tap_of(0, rows), x, pltpu.roll(x, 1, 1), pltpu.roll(x, 2, 1), None, None)
+            y = short_forward(
+                0, rows, 0, tap_of(0, rows), x, pltpu.roll(x, 1, 1), pltpu.roll(x, 2, 1), None, None
+            )
             gm[rows, lanes(0)] = gx[rows, lanes(0)] * y
+
+    def start_tile(t, carry):
+        tap_tile(t)
+        border_tile(t - 1)
         return carry
 
-    lax.fori_loop(0, channels // 64, border_rows, 0)
+    lax.fori_loop(1, tiles, start_tile, 0)
+    border_tile(tiles - 1)
 
     pl.semaphore_wait(barrier, n - 1)
 
@@ -197,36 +214,27 @@
             device_id={"ctx": left}, device_id_type=MESH,
         )
 
-    @pl.when(has_right)
-    def _():
-        rim_copy.start()
-        ph_copy(0).start()
-
-    @pl.when(has_left)
-    def _():
-        col_copy.start()
-        gh_copy(0).start()
-
-    def filt_copy(d):
+    def filt_copy(k):
         return pltpu.make_async_remote_copy(
             src_ref=filt_s, dst_ref=filt_r.at[me], send_sem=filt_sem.at[0], recv_sem=filt_sem.at[1],
-            device_id={"ctx": lax.rem(me + d, n)}, device_id_type=MESH,
-        )
-
-    def send_filt(d, carry):
-        filt_copy(d).start()
-        return carry
-
-    lax.fori_loop(1, n, send_filt, 0)
+            device_id={"ctx": peer(k)}, device_id_type=MESH,
+        )
+
+    for k in range(n - 1):
+        filt_copy(k).start()
+
+    order = [(c + chunks // 2) % chunks for c in range(chunks)]
 
     @pl.when(has_right)
     def _():
-        for c in range(1, chunks):
+        rim_copy.start()
+        for c in order:
             ph_copy(c).start()
 
     @pl.when(has_left)
     def _():
-        for c in range(1, chunks):
+        col_copy.start()
+        for c in order:
             gh_copy(c).start()
 
     for load in loads[8:]:
@@ -246,7 +254,7 @@
                     x = src[rows, lanes(i)]
                     r1, r2 = pltpu.roll(x, 1, 1), pltpu.roll(x, 2, 1)
                     if i > 0 or w > 0:
-                        short[w] = short_forward(taps3[w], x, r1, r2, b1[w], b2[w])
+                        short[w] = short_forward(w, rows, i, taps3[w], x, r1, r2, b1[w], b2[w])
                     b1[w], b2[w] = r1, r2
                 if i < last:
                     kc[rows, lanes(i)] = short[1]
@@ -394,20 +402,14 @@
             term = m * p
             bias_sum = term if bias_sum is None else bias_sum + term
         acc[lax.rem(t, 2), 9, own_rows, :] = bias_sum
-        for w, (src, dst) in enumerate(((qx, out_q), (kx, out_k), (vx, out_v))):
+        for w, src in enumerate((qx, kx, vx)):
             sums = [None] * SHORT
-            tap = tap_of(w, rows)
-            a1 = a2 = None
-            for i in reversed(range(blocks)):
+            for i in range(blocks):
                 g0 = gw[w][i]
-                r1, r2 = pltpu.roll(g0, LANE - 1, 1), pltpu.roll(g0, LANE - 2, 1)
-                shifted = [g0, shift_left(r1, a1, last1), shift_left(r2, a2, last2)]
-                a1, a2 = r1, r2
-                dst[rows, lanes(i)] = tap[0] * shifted[0] + tap[1] * shifted[1] + tap[2] * shifted[2]
-                x = src[rows, lanes(i)]
+                raw[w, rows, lanes(i)] = g0
                 for j in range(SHORT):
-                    term = shifted[j] * x
-                    sums[j] = term if sums[j] is None else sums[j] + term
+                    x = src[rows, lanes(i)] if j == 0 else xs[w, j - 1, rows, lanes(i)]
+                    sums[j] = g0 * x if sums[j] is None else sums[j] + g0 * x
             for j in range(SHORT):
                 acc[lax.rem(t, 2), w * 3 + j, own_rows, :] = sums[j]
             heads[lax.rem(t, 2), w, own_rows, :] = gw[w][0]
@@ -451,33 +453,37 @@
             def _():
                 msg_copy(o).start()
 
-    def main_tile(t, before, ahead):
+    def main_tile(step, before, ahead):
+        t = tile_at(step)
         if ahead:
-            halo_ready((t + 1) * TILE)
-        steps = TILE // GROUP
+            halo_ready(tile_at(step + 1) * TILE)
+        groups = TILE // GROUP
         matmuls(t, 0)
         if before:
-            tile_sums(t - 1)
-        for u in range(steps):
-            if u + 1 < steps:
+            tile_sums(tile_at(step - 1))
+        for u in range(groups):
+            if u + 1 < groups:
                 matmuls(t, u + 1)
             if ahead and u == 2:
-                rims_in(t + 1)
+                rims_in(tile_at(step + 1))
             gradients(t, u)
         if before:
-            send_sums(t - 1)
-
-    def middle_tile(t, carry):
-        main_tile(t, True, True)
+            send_sums(tile_at(step - 1))
+
+    def tile_at(step):
+        return (step + tiles // 2) % tiles
+
+    def middle_tile(step, carry):
+        main_tile(step, True, True)
         return carry
 
-    halo_ready(0)
-    rims_in(0)
+    halo_ready(tile_at(0) * TILE)
+    rims_in(tile_at(0))
     main_tile(0, False, True)
     lax.fori_loop(1, tiles - 1, middle_tile, 0)
     main_tile(tiles - 1, True, False)
-    tile_sums(tiles - 1)
-    send_sums(tiles - 1)
+    tile_sums(tile_at(tiles - 1))
+    send_sums(tile_at(tiles - 1))
 
     edge_copy = pltpu.make_async_remote_copy(
         src_ref=edge_s, dst_ref=edge_r, send_sem=edge_sem.at[0], recv_sem=edge_sem.at[1],
@@ -488,6 +494,26 @@
     def _():
         edge_copy.start()
 
+    def output_rows(t):
+        for u in range(4):
+            rows = pl.ds(pl.multiple_of(t * 64 + u * GROUP, GROUP), GROUP)
+            for w, dst in enumerate((out_q, out_k, out_v)):
+                tap = tap_of(w, rows)
+                a1 = a2 = None
+                for i in reversed(range(blocks)):
+                    g0 = raw[w, rows, lanes(i)]
+                    r1, r2 = pltpu.roll(g0, LANE - 1, 1), pltpu.roll(g0, LANE - 2, 1)
+                    dst[rows, lanes(i)] = (
+                        tap[0] * g0 + tap[1] * shift_left(r1, a1, last1) + tap[2] * shift_left(r2, a2, last2)
+                    )
+                    a1, a2 = r1, r2
+
+    def output_loop(t, carry):
+        output_rows(t)
+        return carry
+
+    lax.fori_loop(0, tiles, output_loop, 0)
+
     msg_r[me] = msg_s[me]
     drain(msg_r.at[others], msg_sem.at[1])
 
@@ -496,17 +522,23 @@
         total = total + msg_r[o]
     tot_s[...] = jnp.concatenate([total[3:6], jnp.zeros((5, LANE), F32)], axis=0)
 
-    def tot_copy(d):
+    def tot_copy(k):
         return pltpu.make_async_remote_copy(
             src_ref=tot_s, dst_ref=tot_r.at[me], send_sem=tot_sem.at[0], recv_sem=tot_sem.at[1],
-            device_id={"ctx": lax.rem(me + d, n)}, device_id_type=MESH,
-        )
-
-    def send_tot(d, carry):
-        tot_copy(d).start()
+            device_id={"ctx": peer(k)}, device_id_type=MESH,
+        )
+
+    for k in range(3):
+        tot_copy(k).start()
+
+    def output_and_send(t, carry):
+        for k in range(4):
+            tot_copy(4 * t + 3 + k).start()
+        output_rows(t + tiles)
         return carry
 
-    lax.fori_loop(1, n, send_tot, 0)
+    lax.fori_loop(0, tiles - 1, output_and_send, 0)
+    output_rows(2 * tiles - 1)
     tot_r[me] = tot_s[...]
     out_filt[...] = lax.dot_general(
         total, flip.astype(F32), (((1,), (0,)), ((), ())),
@@ -593,6 +625,9 @@
     row = pltpu.VMEM((8, channels), F32)
     slots = pltpu.VMEM((n, 8, LANE), F32)
     one = pltpu.VMEM((8, LANE), F32)
+    short_taps, filters, skip_bias = [
+        pltpu.with_memory_space_constraint(x, pltpu.HBM) for x in (short_taps, filters, skip_bias)
+    ]
     outs = pl.pallas_call(
         functools.partial(kernel, n, blocks),
         out_shape=(
@@ -606,6 +641,8 @@
         out_specs=(vmem,) * 7,
         scratch_shapes=[pltpu.VMEM(full, BF)] * 9
         + [
+            pltpu.VMEM((3, channels, length), BF),
+            pltpu.VMEM((3, 2, channels, length), BF),
             pltpu.VMEM((2, 2, blocks * GROUP, LANE), BF),
             pltpu.VMEM((2, 10, TILE, LANE), BF),
             pltpu.VMEM((2, 3, TILE, LANE), BF),

time: 42 us -> 36.7 us (0.87)
  Pallas kernels: 39 us -> 35.9 us
  local copies, waits for them, and re-layouts: 2.1 us -> 0 us
    pallas_call x1, Pallas kernels: 36.7 us -> 33.6 us  [body(): pl.pallas_call(functools.partial(kernel, n, blocks), out_shape=(pltpu.VME...]
    unnamed x6 -> x0, local copies, waits for them, and re-layouts: 2.1 us -> none
where the time goes in v3:
time: 36.7 us; the launch traced here: 36.6 us
  Pallas kernels  35.9 us (98%)
  between operations  0.64 us (2%)
    pallas_call x1, Pallas kernels, body(): pl.pallas_call(functools.partial(kernel, n, blocks), out_shape=(pltpu.VME...  33.6 us
    pallas_call x1, Pallas kernels, body(): pl.pallas_call(functools.partial(finish, blocks), out_shape=tuple((jax.Sh...  2.28 us

profile of v3, /device:TPU:1, one launch (start us, length us, event | category | flops | bytes accessed | tf_op | source)
XLA Modules:
  0.0 36.6 jit_solution(1225973043506139139)
XLA Ops:
  0.6 33.6 %shard_map.118 = (bf16[1024,768]{1,0:T(8,128)(2,1)S(1)}, bf16[1024,768]{1,0:T(8,128)(2,1)S(1)}, bf16[1024,768]{1,0:T(8,128)(2,1)S(1)}, f32[8,1024]{1,0:T(8,128)S...) custom-call(bf16[1024,768]{1,0:T(8,128)(2,1)} %q_hbm.1, bf16[1024,768]{1,0:T(8,128)(2,1)} %k_hbm.1, ...), custom_call_target="tpu_custom_call" | custom-call | tf_op jit(solution)/shard_map/pallas_call | solution.py:631
  34.3 2.3 %shard_map.119 = (bf16[1024,768]{1,0:T(8,128)(2,1)}, bf16[1024,768]{1,0:T(8,128)(2,1)}, bf16[1024,768]{1,0:T(8,128)(2,1)}, f32[3,3,1024]{2,1,0:T(4,128)}, f32[2,128]{1,0:T(2,128)}, /*index=5*/f32[32]{0:T(128)}) custom-call(bf16[1024,768]{1,0:T(8,128)(2,1)S(1)} %get-tuple-element.13.gq, bf16[1024,768]{1,0:T(8,128)(2,1)S(1)} %get-tuple-element.14.gk, ...), custom_call_target="tpu_custom_call" | custom-call | tf_op jit(solution)/shard_map/pallas_call | solution.py:665

commit v4 on v3

--- a/solution.py
+++ b/solution.py
@@ -242,8 +242,8 @@
 
     def forward_rows(t, carry):
         turned = []
-        for u in range(4):
-            rows = pl.ds(pl.multiple_of(t * 64 + u * GROUP, GROUP), GROUP)
+        for u in range(8):
+            rows = pl.ds(pl.multiple_of(t * 128 + u * GROUP, GROUP), GROUP)
             taps3 = [tap_of(w, rows) for w in range(3)]
             b1, b2 = [None] * 3, [None] * 3
             for i in range(blocks):
@@ -265,14 +265,14 @@
                     gm[rows, lanes(i)] = m
                     turned.append(m)
         turned = nn(jnp.concatenate(turned, axis=0), flip).astype(BF)
-        for u in range(4):
-            rows = pl.ds(pl.multiple_of(t * 64 + u * GROUP, GROUP), GROUP)
+        for u in range(8):
+            rows = pl.ds(pl.multiple_of(t * 128 + u * GROUP, GROUP), GROUP)
             for i in range(1, blocks):
                 at = (u * last + i - 1) * GROUP
                 gmr[rows, lanes(i)] = turned[at : at + GROUP]
         return carry
 
-    lax.fori_loop(0, channels // 64, forward_rows, 0)
+    lax.fori_loop(0, channels // 128, forward_rows, 0)
 
     @pl.when(has_left)
     def _():
@@ -462,11 +462,11 @@
         if before:
             tile_sums(tile_at(step - 1))
         for u in range(groups):
+            gradients(t, u)
             if u + 1 < groups:
                 matmuls(t, u + 1)
             if ahead and u == 2:
                 rims_in(tile_at(step + 1))
-            gradients(t, u)
         if before:
             send_sums(tile_at(step - 1))
 
@@ -512,7 +512,8 @@
         output_rows(t)
         return carry
 
-    lax.fori_loop(0, tiles, output_loop, 0)
+    early_rows = 2 * tiles - tiles // 2
+    lax.fori_loop(0, early_rows, output_loop, 0)
 
     msg_r[me] = msg_s[me]
     drain(msg_r.at[others], msg_sem.at[1])
@@ -528,17 +529,10 @@
             device_id={"ctx": peer(k)}, device_id_type=MESH,
         )
 
-    for k in range(3):
+    for k in range(n - 1):
         tot_copy(k).start()
 
-    def output_and_send(t, carry):
-        for k in range(4):
-            tot_copy(4 * t + 3 + k).start()
-        output_rows(t + tiles)
-        return carry
-
-    lax.fori_loop(0, tiles - 1, output_and_send, 0)
-    output_rows(2 * tiles - 1)
+    lax.fori_loop(early_rows, 2 * tiles, output_loop, 0)
     tot_r[me] = tot_s[...]
     out_filt[...] = lax.dot_general(
         total, flip.astype(F32), (((1,), (0,)), ((), ())),

time: 36.7 us -> 36.1 us (0.984)
  Pallas kernels: 35.9 us -> 35.4 us
    pallas_call x1, Pallas kernels: 33.6 us -> 33.1 us  [body(): pl.pallas_call(functools.partial(kernel, n, blocks), out_shape=(pltpu.VME...]
where the time goes in v4:
time: 36.1 us; the launch traced here: 36 us
  Pallas kernels  35.4 us (98%)
  between operations  0.64 us (2%)
    pallas_call x1, Pallas kernels, body(): pl.pallas_call(functools.partial(kernel, n, blocks), out_shape=(pltpu.VME...  33.1 us
    pallas_call x1, Pallas kernels, body(): pl.pallas_call(functools.partial(finish, blocks), out_shape=tuple((jax.Sh...  2.28 us

profile of v4, /device:TPU:1, one launch (start us, length us, event | category | flops | bytes accessed | tf_op | source)
XLA Modules:
  0.0 36.0 jit_solution(1230838167789594881)
XLA Ops:
  0.6 33.1 %shard_map.118 = (bf16[1024,768]{1,0:T(8,128)(2,1)S(1)}, bf16[1024,768]{1,0:T(8,128)(2,1)S(1)}, bf16[1024,768]{1,0:T(8,128)(2,1)S(1)}, f32[8,1024]{1,0:T(8,128)S...) custom-call(bf16[1024,768]{1,0:T(8,128)(2,1)} %q_hbm.1, bf16[1024,768]{1,0:T(8,128)(2,1)} %k_hbm.1, ...), custom_call_target="tpu_custom_call" | custom-call | tf_op jit(solution)/shard_map/pallas_call | solution.py:625
  33.7 2.3 %shard_map.119 = (bf16[1024,768]{1,0:T(8,128)(2,1)}, bf16[1024,768]{1,0:T(8,128)(2,1)}, bf16[1024,768]{1,0:T(8,128)(2,1)}, f32[3,3,1024]{2,1,0:T(4,128)}, f32[2,128]{1,0:T(2,128)}, /*index=5*/f32[32]{0:T(128)}) custom-call(bf16[1024,768]{1,0:T(8,128)(2,1)S(1)} %get-tuple-element.13.gq, bf16[1024,768]{1,0:T(8,128)(2,1)S(1)} %get-tuple-element.14.gk, ...), custom_call_target="tpu_custom_call" | custom-call | tf_op jit(solution)/shard_map/pallas_call | solution.py:659

commit v5 on v4

--- a/solution.py
+++ b/solution.py
@@ -73,6 +73,10 @@
         z, x, c = (me // 8 + dz) % 4, (me // 2 + dx) % 4, (me + 1 + k % 2) % 2
         return z * 8 + x * 2 + c
 
+    barrier = pltpu.get_barrier_semaphore()
+    for k in range(n - 1):
+        pl.semaphore_signal(barrier, inc=1, device_id={"ctx": peer(k)}, device_id_type=MESH)
+
     def piece(i, src, dst, start, size):
         cols = pl.ds(start * LANE, size * LANE)
         return pltpu.make_async_copy(src.at[:, cols], dst.at[:, cols], in_sem.at[i])
@@ -93,16 +97,6 @@
     ]
     for load in loads:
         load.start()
-
-    barrier = pltpu.get_barrier_semaphore()
-
-    def greet(d, carry):
-        pl.semaphore_signal(
-            barrier, inc=1, device_id={"ctx": lax.rem(me + d, n)}, device_id_type=MESH
-        )
-        return carry
-
-    lax.fori_loop(1, n, greet, 0)
 
     lane16 = iota((GROUP, LANE), 1)
     first1, first2 = lane16 < 1, lane16 < 2

time: 36.1 us -> 36.5 us (1.011)
  no operation moved by 1% of the time
where the time goes in v5:
time: 36.5 us; the launch traced here: 36.4 us
  Pallas kernels  35.7 us (98%)
  between operations  0.64 us (2%)
    pallas_call x1, Pallas kernels, body(): pl.pallas_call(functools.partial(kernel, n, blocks), out_shape=(pltpu.VME...  33.4 us
    pallas_call x1, Pallas kernels, body(): pl.pallas_call(functools.partial(finish, blocks), out_shape=tuple((jax.Sh...  2.28 us

profile of v5, /device:TPU:1, one launch (start us, length us, event | category | flops | bytes accessed | tf_op | source)
XLA Modules:
  0.0 36.4 jit_solution(2390808488253849366)
XLA Ops:
  0.6 33.4 %shard_map.118 = (bf16[1024,768]{1,0:T(8,128)(2,1)S(1)}, bf16[1024,768]{1,0:T(8,128)(2,1)S(1)}, bf16[1024,768]{1,0:T(8,128)(2,1)S(1)}, f32[8,1024]{1,0:T(8,128)S...) custom-call(bf16[1024,768]{1,0:T(8,128)(2,1)} %q_hbm.1, bf16[1024,768]{1,0:T(8,128)(2,1)} %k_hbm.1, ...), custom_call_target="tpu_custom_call" | custom-call | tf_op jit(solution)/shard_map/pallas_call | solution.py:619
  34.1 2.3 %shard_map.119 = (bf16[1024,768]{1,0:T(8,128)(2,1)}, bf16[1024,768]{1,0:T(8,128)(2,1)}, bf16[1024,768]{1,0:T(8,128)(2,1)}, f32[3,3,1024]{2,1,0:T(4,128)}, f32[2,128]{1,0:T(2,128)}, /*index=5*/f32[32]{0:T(128)}) custom-call(bf16[1024,768]{1,0:T(8,128)(2,1)S(1)} %get-tuple-element.13.gq, bf16[1024,768]{1,0:T(8,128)(2,1)S(1)} %get-tuple-element.14.gk, ...), custom_call_target="tpu_custom_call" | custom-call | tf_op jit(solution)/shard_map/pallas_call | solution.py:653
